TPU v7x, 32 devices: a whole 2x2x4 slice. The times are simulated.
32 devices in a mesh: groups: 2 (over y), tensor: 4 (over z), dp: 2 (over x), seq: 2 (over core).
Axes of the slice: x: 2, y: 2, z: 4, core: 2. Of those that a mesh axis runs over, the one named last changes fastest.
Arguments:
- out_grad: bfloat16 [4096, 4096], P(('groups', 'dp', 'seq'), 'tensor'), parts along dimension 0, may hold values from -6 to 6
- layer_in: bfloat16 [4096, 4096], P(('groups', 'dp', 'seq'), 'tensor'), parts along dimension 0, may hold values from -6 to 6
- gate_pre: bfloat16 [4096, 14336], P(('groups', 'dp', 'seq'), 'tensor'), parts along dimension 0, may hold values from -8 to 8
- down_weight: bfloat16 [14336, 4096], P('tensor'), may hold values from -0.09375 to 0.09375
- proj_in: bfloat16 [4096, 64], P('tensor'), may hold values from -0.09375 to 0.09375
- proj_out: bfloat16 [14336, 64], P('tensor'), may hold values from -0.046875 to 0.046875
- segment_ids: int32 [4, 1024], P(('groups', 'dp'), 'seq'), parts along dimension 0, may hold values from 0 to 3, never falling along the last dimension, each value on 1 to 512 neighbouring positions
- query_bank: bfloat16 [256, 4096], P(('groups', 'dp')), parts along dimension 0, may hold values from -6 to 6
- query_ids: int32 [512], P('groups'), parts along dimension 0, may hold values from 0 to 127
Outputs:
- scores: float32 [16, 256], P(('groups', 'dp')), parts along dimension 0
There are 2 independent parts, one for each index of `groups`. A program takes and returns all parts, laid end to end along the dimension named above; an argument that names none is the same for every part. Nothing has to cross between parts.
Inputs may be any that keep to these rules, and one draw needn't show every extreme that they name: `segment_ids`: ids never fall along a row; every id of a row occurs; one example of a row has exactly 512 tokens.
All inputs are finite; a program needn't handle non-finite values.
Results may differ from a plain program's by a relative error of at most 0.003.
Values may be sent and summed in bfloat16 or wider, within the bound.
No kernel may reach another device: no remote copies, remote signals or barrier semaphores. Data moves between devices by JAX's collectives and lax.ppermute only.
A program may use at most 128 MiB of HBM per device.

v0:
```python
import jax
import jax.numpy as jnp
from jax import lax
from jax.sharding import PartitionSpec as P

EX_DEV = 4


exact_precision = lax.Precision.HIGHEST


def local_sketch(stacked, seg_rows, proj_width):
    count_rows = stacked.shape[0]
    onehot = (seg_rows[:, None] == jnp.arange(EX_DEV, dtype=jnp.int32)[None, :]).astype(jnp.float32)
    out_rows = stacked[:, :proj_width]
    in_rows = stacked[:, proj_width:]
    weighted = (onehot[:, :, None] * out_rows[:, None, :]).reshape(count_rows, EX_DEV * proj_width)
    partial_value = lax.dot_general(
        weighted, in_rows, (((0,), (0,)), ((), ())), precision=exact_precision
    )
    return partial_value.reshape(EX_DEV, proj_width * proj_width)


def body(
    out_grad, layer_in, gate_pre, down_weight, proj_in, proj_out, segment_ids, query_bank, query_ids
):
    proj_width = proj_in.shape[1]
    hidden_grad = lax.dot_general(
        lax.all_gather(out_grad, "tensor", axis=1, tiled=True),
        down_weight,
        (((1,), (1,)), ((), ())),
        preferred_element_type=jnp.float32,
    )
    up_grad = (hidden_grad * jax.nn.silu(gate_pre.astype(jnp.float32))).astype(jnp.bfloat16)
    seg_local = segment_ids.reshape(-1)
    out_term = jnp.dot(up_grad, proj_out, preferred_element_type=jnp.float32)
    in_term = jnp.dot(layer_in, proj_in, preferred_element_type=jnp.float32)
    stacked = jnp.concatenate([out_term, in_term], axis=1)
    summed = lax.psum(stacked, "tensor")
    partial_value = local_sketch(summed, seg_local, proj_width)
    sketch = lax.psum(partial_value, "seq")
    portion = lax.all_gather(query_bank, "dp", axis=0, tiled=True)
    bank_scores = jnp.dot(sketch, portion.astype(jnp.float32).T, precision=exact_precision)
    chooser = (query_ids[None, :] == jnp.arange(portion.shape[0], dtype=jnp.int32)[:, None]).astype(
        jnp.float32
    )
    scores = jnp.dot(bank_scores, chooser, precision=exact_precision)
    return scores * (1.0 / (8.0 * proj_width))


def solution(mesh):
    in_specs = (
        P(("groups", "dp", "seq"), "tensor"),
        P(("groups", "dp", "seq"), "tensor"),
        P(("groups", "dp", "seq"), "tensor"),
        P("tensor", None),
        P("tensor", None),
        P("tensor", None),
        P(("groups", "dp"), "seq"),
        P(("groups", "dp"), None),
        P("groups"),
    )
    out_specs = P(("groups", "dp"), None)
    return jax.shard_map(body, mesh=mesh, in_specs=in_specs, out_specs=out_specs, check_vma=False)
```

profile of v0, /device:TPU:0, one launch (start us, length us, event | category | flops | bytes accessed | tf_op | source)
XLA Modules:
  0.0 183.9 jit_solution(17015475335776646261)
XLA Ops:
  7.4 0.0 copy-start
  7.4 0.0 all-gather.3.cloned.1.call-start
  7.4 0.7 all-gather.3.cloned.1.call-update
  8.1 0.0 all-reduce.3.cloned.1.call-start
  8.1 0.5 copy-done
  8.6 1.3 fusion.10
  9.9 0.0 copy-start.1
  9.9 0.0 copy-start.2
  10.0 83.3 %all-gather.3.cloned.1.call-done = bf16[512,4096]{1,0:T(8,128)(2,1)} async-done(((bf16[512,1024]{1,0:T(8,128)(2,1)}), bf16[512,4096]{1,0:T(8,128)(2,1)}) %all-gather.3.cloned.1.call-update) | async-done | bytes 4194320 | tf_op jit(solution)/shard_map/all_gather | solution.py:29
  93.3 25.0 %fusion.9 = f32[512,64]{0,1:T(8,128)S(1)} fusion(bf16[3584,64]{0,1:T(8,128)(2,1)} %param.14, bf16[512,3584]{1,0:T(8,128)(2,1)} %param.11, bf16[512,4096]{1,0:T(8,128)(2,1)} %all-gather.3.cloned.1.call-done, bf16[3584,4096]{1,0:T(8,128)(2,1)} %param.12), kind=kOutput, calls=%fused_computation.16 | convolution fusion | flops 15280111616 | bytes 37814272 | tf_op jit(solution)/shard_map/dot_general | solution.py:36
  118.3 0.7 pad_maximum_fusion
  119.0 0.0 all-reduce.3.cloned.1.call-update
  119.0 0.0 all-gather.5.cloned.1.call-start
  119.1 0.5 all-gather.5.cloned.1.call-update
  119.6 0.0 all-reduce.5.cloned.1.call-start
  119.7 0.0 copy-done.1
  119.7 33.3 %all-reduce.3.cloned.1.call-done = f32[512,128]{0,1:T(8,128)} async-done(((f32[512,128]{0,1:T(8,128)}), f32[512,128]{0,1:T(8,128)}) %all-reduce.3.cloned.1.call-update) | async-done | bytes 262160 | tf_op jit(solution)/shard_map/psum | solution.py:39
  153.0 0.9 slice.8
  153.9 0.1 broadcast_multiply_fusion
  154.0 1.5 fusion.5
  155.5 0.7 reshape.34
  156.2 0.0 all-reduce.5.cloned.1.call-update
  156.2 0.0 all-gather.5.cloned.1.call-done
  156.3 17.6 %all-reduce.5.cloned.1.call-done = f32[4,4096]{1,0:T(4,128)} async-done(((f32[4,4096]{1,0:T(4,128)}), f32[4,4096]{1,0:T(4,128)}) %all-reduce.5.cloned.1.call-update) | async-done | bytes 65552 | tf_op jit(solution)/shard_map/psum | solution.py:41
  173.8 2.2 %fusion.11 = f32[4,128]{1,0:T(4,128)S(1)} fusion(f32[4,4096]{1,0:T(4,128)} %all-reduce.5.cloned.1.call-done, bf16[128,4096]{1,0:T(8,128)(2,1)} %all-gather.5.cloned.1.call-done), kind=kOutput, calls=%fused_computation.18 | convolution fusion | flops 25165824 | bytes 1116160 | tf_op jit(solution)/shard_map/dot_general | solution.py:43
  176.0 0.0 copy-done.2
  176.0 0.8 convolution_multiply_fusion
  (1 shorter events, 0.0 us)
Async XLA Ops:
  7.4 1.2 copy-start
  7.4 85.9 %all-gather.3.cloned.1.call-start = ((), (), s32[]{:S(2)}) async-start(), calls=%async_computation | async-start | bytes 5242880 | tf_op jit(solution)/shard_map/all_gather | solution.py:29
  8.1 144.9 %all-reduce.3.cloned.1.call-start = ((), (), s32[]{:S(2)}) async-start(), calls=%async_computation.1 | async-start | bytes 524288 | tf_op jit(solution)/shard_map/psum | solution.py:39
  9.9 109.7 %copy-start.1 = (s32[1,512]{1,0:T(1,128)S(1)}, s32[1,512]{1,0:T(1,128)}, u32[]{:S(2)}) copy-start(s32[1,512]{1,0:T(1,128)} %param.15) | copy-start | bytes 6148
  9.9 166.1 %copy-start.2 = (s32[256]{0:T(256)S(1)}, s32[256]{0:T(256)}, u32[]{:S(2)}) copy-start(s32[256]{0:T(256)} %param.17) | copy-start | bytes 3076
  119.0 37.2 %all-gather.5.cloned.1.call-start = ((), (), s32[]{:S(2)}) async-start(), calls=%async_computation.3 | async-start | bytes 1572864 | tf_op jit(solution)/shard_map/all_gather | solution.py:42
  119.6 54.2 %all-reduce.5.cloned.1.call-start = ((), (), s32[]{:S(2)}) async-start(), calls=%async_computation.2 | async-start | bytes 131072 | tf_op jit(solution)/shard_map/psum | solution.py:41
Sparse Core Ops, SparseCore 0:
  9.8 83.4 all-gather.2
  119.1 33.8 all-reduce.2
  156.4 17.4 all-reduce.4
Sparse Core Ops, SparseCore 1:
  121.1 19.7 all-gather.4
where the time goes:
time: 184 us
  waiting for transfers between devices  135 us (73%)
  matrix products  30.8 us (17%)
  between operations  14.6 us (8%)
  local copies, waits for them, and re-layouts  2.12 us (1%)
    all_gather x1, waiting for transfers between devices, body(): lax.all_gather(out_grad, 'tensor', axis=1, tiled=True)  83.3 us
    psum x1, waiting for transfers between devices, body(): summed = lax.psum(stacked, 'tensor')  33.3 us
    dot_general x1, matrix products, body(): out_term = jnp.dot(up_grad, proj_out, preferred_element_type=jnp.float32)  25 us
    psum x1, waiting for transfers between devices, body(): sketch = lax.psum(partial_value, 'seq')  17.6 us
  transfers between devices with their start and end apart: 4, of which 3 were waited for; matrix products, arithmetic and copies ran while one was open for 2% of the time, Pallas kernels for 0%

commit v1 on v0

v1 whole, which is shorter than its diff:
```python
import functools

import jax
import jax.numpy as jnp
from jax import lax
from jax.experimental import pallas as pl
from jax.experimental.pallas import tpu as pltpu
from jax.sharding import PartitionSpec as P

EX_DEV = 4
EXACT = lax.Precision.HIGHEST
NT = (((1,), (1,)), ((), ()))


def after(value, *deps):
    return lax.optimization_barrier((value, *deps))[0]


def sum_over(value, axis, size):
    step = 1
    while step < size:
        value = value + lax.ppermute(value, axis, [(i, i ^ step) for i in range(size)])
        step *= 2
    return value


def tile_of(count, largest):
    return max((t for t in range(128, largest + 1, 128) if count % t == 0), default=count)


def hidden_kernel(blocks, place_ref, *refs):
    parts, weights, total_ref = refs[:blocks], refs[blocks : 2 * blocks], refs[-1]
    total = lax.dot_general(parts[0][...], weights[0][...], NT, preferred_element_type=jnp.float32)
    for part, weight in zip(parts[1:], weights[1:]):
        total += lax.dot_general(part[...], weight[...], NT, preferred_element_type=jnp.float32)
    total_ref[...] = total


def hidden_sum(parts, places, weight):
    tokens, width = parts[0].shape
    hidden = weight.shape[0]
    tile = tile_of(hidden, 512)
    blocks = len(parts)
    return pl.pallas_call(
        functools.partial(hidden_kernel, blocks),
        grid_spec=pltpu.PrefetchScalarGridSpec(
            num_scalar_prefetch=1,
            grid=(hidden // tile,),
            in_specs=[pl.BlockSpec((tokens, width), lambda f, place: (0, 0))] * blocks
            + [pl.BlockSpec((tile, width), lambda f, place, k=k: (f, place[k])) for k in range(blocks)],
            out_specs=pl.BlockSpec((tokens, tile), lambda f, place: (0, f)),
        ),
        out_shape=jax.ShapeDtypeStruct((tokens, hidden), jnp.float32),
        compiler_params=pltpu.CompilerParams(vmem_limit_bytes=24 << 20),
        cost_estimate=pl.CostEstimate(
            flops=2 * blocks * tokens * width * hidden,
            bytes_accessed=2 * blocks * width * (tokens + hidden) + 4 * tokens * hidden,
            transcendentals=0,
        ),
    )(places, *parts, *([weight] * blocks))


def last_kernel(
    scale, place_ref, part_ref, weight_ref, total_ref, gate_ref, proj_ref, inside_ref, bank_ref, pick_ref,
    scores_ref, out_ref, sketch_ref, flat_ref,
):
    step = pl.program_id(0)
    hidden = total_ref[...] + lax.dot_general(
        part_ref[...], weight_ref[...], NT, preferred_element_type=jnp.float32
    )
    gate = gate_ref[...].astype(jnp.float32)
    up = (hidden * (gate / (1.0 + jnp.exp(-gate)))).astype(jnp.bfloat16)
    term = jnp.dot(up, proj_ref[...], preferred_element_type=jnp.float32)

    @pl.when(step == 0)
    def _():
        out_ref[...] = term

    @pl.when(step > 0)
    def _():
        out_ref[...] += term

    @pl.when(step == pl.num_programs(0) - 1)
    def _():
        rows = inside_ref.shape[0] // EX_DEV
        half = out_ref.shape[1] // 2
        sketch_ref[...] = jnp.dot(
            inside_ref[...], out_ref[...], precision=EXACT, preferred_element_type=jnp.float32
        )
        left = lax.broadcasted_iota(jnp.int32, (EX_DEV, 2 * half), 1) < half
        for pair in range(rows // 2):
            first = sketch_ref[pl.ds(2 * pair, EX_DEV, stride=rows), :]
            second = sketch_ref[pl.ds(2 * pair + 1, EX_DEV, stride=rows), :]
            flat_ref[:, 2 * half * pair : 2 * half * (pair + 1)] = jnp.where(left, first, second)
        flat = flat_ref[...]
        high = flat.astype(jnp.bfloat16)
        rest = flat - high.astype(jnp.float32)
        mid = rest.astype(jnp.bfloat16)
        low = (rest - mid.astype(jnp.float32)).astype(jnp.bfloat16)
        bank = bank_ref[...]
        found = sum(lax.dot_general(t, bank, NT, preferred_element_type=jnp.float32) for t in (high, mid, low))
        scores_ref[...] = scale * jnp.dot(
            found, pick_ref[...], precision=EXACT, preferred_element_type=jnp.float32
        )


def last_scores(part, place, weight, total, gate, proj, inside, bank, pick, scale):
    tokens, width = part.shape
    hidden = weight.shape[0]
    tile = tile_of(hidden, 512)
    whole = lambda a: pl.BlockSpec(a.shape, lambda f, place: (0,) * a.ndim)
    return pl.pallas_call(
        functools.partial(last_kernel, scale),
        grid_spec=pltpu.PrefetchScalarGridSpec(
            num_scalar_prefetch=1,
            grid=(hidden // tile,),
            in_specs=[
                whole(part),
                pl.BlockSpec((tile, width), lambda f, place: (f, place[0])),
                pl.BlockSpec((tokens, tile), lambda f, place: (0, f)),
                pl.BlockSpec((tokens, tile), lambda f, place: (0, f)),
                pl.BlockSpec((tile, proj.shape[1]), lambda f, place: (f, 0)),
                whole(inside),
                whole(bank),
                whole(pick),
            ],
            out_specs=pl.BlockSpec((EX_DEV, pick.shape[1]), lambda f, place: (0, 0)),
            scratch_shapes=[
                pltpu.VMEM((tokens, proj.shape[1]), jnp.float32),
                pltpu.VMEM((inside.shape[0], proj.shape[1]), jnp.float32),
                pltpu.VMEM((EX_DEV, bank.shape[1]), jnp.float32),
            ],
        ),
        out_shape=jax.ShapeDtypeStruct((EX_DEV, pick.shape[1]), jnp.float32),
        compiler_params=pltpu.CompilerParams(vmem_limit_bytes=28 << 20),
        cost_estimate=pl.CostEstimate(
            flops=2 * tokens * width * hidden,
            bytes_accessed=2 * width * (tokens + hidden) + 6 * tokens * hidden,
            transcendentals=tokens * hidden,
        ),
    )(place, part, weight, total, gate, proj, inside, bank, pick)


def whole_bank(query_bank, query_ids, size):
    me = lax.axis_index("dp")
    held = query_bank.shape[0]
    rows = jnp.arange(held, dtype=jnp.int32)
    parts, places = [query_bank], [me * held + rows]
    for k in range(1, size):
        parts.append(lax.ppermute(query_bank, "dp", [(i, (i + k) % size) for i in range(size)]))
        places.append((me - k) % size * held + rows)
    pick = (jnp.concatenate(places)[:, None] == query_ids[None, :]).astype(jnp.float32)
    return jnp.concatenate(parts), pick


def body(
    sizes, out_grad, layer_in, gate_pre, down_weight, proj_in, proj_out, segment_ids, query_bank, query_ids
):
    tensor = sizes["tensor"]
    me = lax.axis_index("tensor")
    width = proj_in.shape[1]
    scale = 1.0 / (8.0 * width)

    send = lambda value, pairs: lax.ppermute(value, "tensor", pairs)
    if tensor == 4:
        near = send(out_grad, [(0, 1), (1, 0), (2, 3), (3, 2)])
        middle = send(out_grad, [(1, 2), (2, 1), (0, 0), (3, 3)])
        cross = send(out_grad, [(0, 3), (3, 0)])
        far = send(middle, [(0, 2), (2, 3), (3, 1), (1, 0)])
        rest = jnp.where((me == 0) | (me == 3), cross, middle)
        parts = [out_grad, near, far]
        pick_of = lambda *t: jnp.asarray(t, jnp.int32)[me]
        places = jnp.stack([me, me ^ 1, pick_of(2, 3, 0, 1)]).astype(jnp.int32)
        place = pick_of(3, 2, 1, 0)[None]
    else:
        gathered = lax.all_gather(out_grad, "tensor", axis=1, tiled=True)
        step = gathered.shape[1] // 2
        parts, rest = [gathered[:, :step]], gathered[:, step:]
        places, place = jnp.zeros((1,), jnp.int32), jnp.ones((1,), jnp.int32)

    in_part = lax.dot_general(proj_in, layer_in, (((0,), (1,)), ((), ())), preferred_element_type=jnp.float32)
    in_sum = sum_over(in_part, "tensor", tensor)
    seg = segment_ids.reshape(-1)
    inside = jnp.concatenate([jnp.where(seg[None, :] == n, in_sum, 0.0) for n in range(EX_DEV)])
    bank, pick = whole_bank(query_bank, query_ids, sizes["dp"])
    stored = bank.shape[0]
    bank = bank.reshape(stored, width, width).swapaxes(1, 2).reshape(stored, width * width)
    proj = jnp.concatenate([proj_out, proj_out], axis=1)

    total = hidden_sum(parts, places, down_weight)
    scores = last_scores(rest, place, down_weight, total, gate_pre, proj, inside, bank, pick, scale)
    scores = sum_over(scores, "seq", sizes["seq"])
    return sum_over(scores, "tensor", tensor)


def solution(mesh):
    in_specs = (
        P(("groups", "dp", "seq"), "tensor"),
        P(("groups", "dp", "seq"), "tensor"),
        P(("groups", "dp", "seq"), "tensor"),
        P("tensor", None),
        P("tensor", None),
        P("tensor", None),
        P(("groups", "dp"), "seq"),
        P(("groups", "dp"), None),
        P("groups"),
    )
    out_specs = P(("groups", "dp"), None)
    sizes = {name: mesh.shape[name] for name in mesh.axis_names}
    return jax.shard_map(
        functools.partial(body, sizes), mesh=mesh, in_specs=in_specs, out_specs=out_specs, check_vma=False
    )
```

time: 184 us -> 139 us (0.76)
  waiting for transfers between devices: 135 us -> 62.2 us
  matrix products: 30.8 us -> 1.34 us
  Pallas kernels: 0 us -> 29.4 us
  starting transfers between devices: 0.13 us -> 27.1 us
  between operations: 14.6 us -> 0.22 us
  other arithmetic: 0.77 us -> 8.54 us
  local copies, waits for them, and re-layouts: 2.12 us -> 8.68 us
    all_gather x2 -> x0, waiting for transfers between devices: 83.3 us -> none  [the longest x1 83.3 us: body(): lax.all_gather(out_grad, 'tensor', axis=1, tiled=True)]
    ppermute x0 -> x10, waiting for transfers between devices: none -> 62.2 us  [the longest x5 46.7 us: sum_over(): lax.ppermute(value, axis, [(i, i ^ step) for i in range(size)])]
    psum x2 -> x0, waiting for transfers between devices: 50.9 us -> none  [the longest x1 33.3 us: body(): summed = lax.psum(stacked, 'tensor')]
    dot_general x5 -> x1, matrix products: 30.8 us -> 1.34 us  [body(): lax.dot_general(proj_in, layer_in, (((0,), (1,)), ((), ())), preferred_el...]
    pallas_call x0 -> x2, Pallas kernels: none -> 29.4 us  [the longest x1 17.1 us: hidden_sum(): pl.pallas_call(functools.partial(hidden_kernel, blocks), grid_spec=pltpu....]
    ppermute x0 -> x10, starting transfers between devices: none -> 27.1 us  [the longest x4 16.7 us: body(): send = lambda value, pairs: lax.ppermute(value, 'tensor', pairs)]
    select_n x0 -> x3, other arithmetic: none -> 2.45 us  [the longest x1 1.43 us: body(): rest = jnp.where((me == 0) | (me == 3), cross, middle)]
    ppermute x0 -> x1, local copies, waits for them, and re-layouts: none -> 2.36 us  [whole_bank(): lax.ppermute(query_bank, 'dp', [(i, (i + k) % size) for i in range(size)])]
  transfers between devices with their start and end apart: 4 -> 10, of which waited for: 3 -> 6; matrix products, arithmetic and copies ran while one was open for 2% -> 13% of each run, Pallas kernels for 0% -> 0%
where the time goes in v1:
time: 139 us; the launch traced here: 138 us
  waiting for transfers between devices  62.2 us (45%)
  Pallas kernels  29.4 us (21%)
  starting transfers between devices  27.1 us (19%)
  local copies, waits for them, and re-layouts  8.68 us (6%)
  other arithmetic  8.54 us (6%)
    ppermute x5, waiting for transfers between devices, sum_over(): lax.ppermute(value, axis, [(i, i ^ step) for i in range(size)])  46.7 us
    pallas_call x1, Pallas kernels, hidden_sum(): pl.pallas_call(functools.partial(hidden_kernel, blocks), grid_spec=pltpu....  17.1 us
    ppermute x4, starting transfers between devices, body(): send = lambda value, pairs: lax.ppermute(value, 'tensor', pairs)  16.7 us
    ppermute x4, waiting for transfers between devices, body(): send = lambda value, pairs: lax.ppermute(value, 'tensor', pairs)  15.5 us
    pallas_call x1, Pallas kernels, last_scores(): pl.pallas_call(functools.partial(last_kernel, scale), grid_spec=pltpu.Pre...  12.4 us
    ppermute x5, starting transfers between devices, sum_over(): lax.ppermute(value, axis, [(i, i ^ step) for i in range(size)])  8.84 us
  transfers between devices with their start and end apart: 10, of which 6 were waited for; matrix products, arithmetic and copies ran while one was open for 13% of the time, Pallas kernels for 0%

profile of v1, /device:TPU:0, one launch (start us, length us, event | category | flops | bytes accessed | tf_op | source)
XLA Modules:
  0.0 137.5 jit_solution(731573609395018454)
XLA Ops:
  0.0 9.6 %collective-permute-start.1 = (bf16[512,1024]{1,0:T(8,128)(2,1)}, bf16[512,1024]{1,0:T(8,128)(2,1)}, u32[]{:S(2)}, u32[]{:S(2)}) collective-permute-start(bf16[512,1024]{1,0:T(8,128)(2,1)} %refs_0_.1), channel_id=1, source_target_pairs={{4,8},{8,4},{0,0},{12,12},{5,9},{9,5},{1,1},{13,13},{6,10},{10,6},... | collective-permute-start | bytes 3145736 | tf_op jit(solution)/shard_map/ppermute | solution.py:164
  9.6 0.0 collective-permute-start.2
  9.6 7.0 %collective-permute-start = (bf16[512,1024]{1,0:T(8,128)(2,1)}, bf16[512,1024]{1,0:T(8,128)(2,1)}, u32[]{:S(2)}, u32[]{:S(2)}) collective-permute-start(bf16[512,1024]{1,0:T(8,128)(2,1)} %refs_0_.1), channel_id=1, source_target_pairs={{0,12},{12,0},{1,13},{13,1},{2,14},{14,2},{3,15},{15,3},{16,28},{2... | collective-permute-start | bytes 3145736 | tf_op jit(solution)/shard_map/ppermute | solution.py:164
  16.6 0.0 copy-done
  16.6 1.3 fusion
  17.9 0.0 copy-start.4
  17.9 0.1 collective-permute-start.4
  18.0 1.6 %collective-permute-start.6 = (bf16[64,4096]{1,0:T(8,128)(2,1)}, bf16[64,4096]{1,0:T(8,128)(2,1)}, u32[]{:S(2)}, u32[]{:S(2)}) collective-permute-start(bf16[64,4096]{1,0:T(8,128)(2,1)} %param.18), channel_id=1, source_target_pairs={{0,2},{2,0},{1,3},{3,1},{4,6},{6,4},{5,7},{7,5},{8,10},{10,8},{9,1... | collective-permute-start | bytes 1572872 | tf_op jit(solution)/shard_map/ppermute | solution.py:150
  19.6 1.4 %copy.21 = bf16[3584,64]{1,0:T(8,128)(2,1)S(1)} copy(bf16[3584,64]{0,1:T(8,128)(2,1)} %param.16) | data formatting | bytes 917504 | tf_op args[5]
  21.0 0.0 copy-start.7
  21.0 0.0 copy-start.5
  21.1 0.1 pad_add_fusion.1
  21.1 0.6 dynamic_slice.7
  21.7 0.5 pad_maximum_fusion.1.proj_ref
  22.3 0.7 compare_convert_fusion.pick_ref
  23.0 37.0 %collective-permute-done.4 = f32[64,512]{1,0:T(8,128)} collective-permute-done((f32[64,512]{1,0:T(8,128)S(1)}, f32[64,512]{1,0:T(8,128)}, u32[]{:S(2)}, u32[]{:S(2)}) %collective-permute-start.4) | collective-permute-done | bytes 131104 | tf_op jit(solution)/shard_map/ppermute | solution.py:22
  60.0 1.6 %add.37 = f32[64,512]{1,0:T(8,128)} add(f32[64,512]{1,0:T(8,128)S(1)} %fusion, f32[64,512]{1,0:T(8,128)} %collective-permute-done.4) | non-fusion elementwise | flops 32768 | bytes 393216 | tf_op jit(solution)/shard_map/add | solution.py:22
  61.6 4.0 %collective-permute-start.5 = (f32[64,512]{1,0:T(8,128)}, f32[64,512]{1,0:T(8,128)}, u32[]{:S(2)}, u32[]{:S(2)}) collective-permute-start(f32[64,512]{1,0:T(8,128)} %add.37), channel_id=1, source_target_pairs={{0,8},{4,12},{8,0},{12,4},{1,9},{5,13},{9,1},{13,5},{2,10},{6,14},... | collective-permute-start | bytes 393224 | tf_op jit(solution)/shard_map/ppermute | solution.py:22
  65.5 0.7 pad_add_fusion.place_ref
  66.2 0.0 copy-done.4
  66.3 0.5 copy.23
  66.8 0.6 dynamic_slice.6.place_ref
  67.4 0.0 copy-done.5
  67.4 4.2 %collective-permute-done.5 = f32[64,512]{1,0:T(8,128)} collective-permute-done((f32[64,512]{1,0:T(8,128)}, f32[64,512]{1,0:T(8,128)}, u32[]{:S(2)}, u32[]{:S(2)}) %collective-permute-start.5) | collective-permute-done | bytes 131104 | tf_op jit(solution)/shard_map/ppermute | solution.py:22
  71.6 1.0 broadcast_select_fusion.4
  72.6 0.0 collective-permute-done.1
  72.6 0.2 collective-permute-start.3
  72.9 0.0 collective-permute-done.6
  72.9 2.4 %copy.24 = bf16[64,4096]{0,1:T(8,128)(2,1)} copy(bf16[64,4096]{1,0:T(8,128)(2,1)} %collective-permute-done.6) | data formatting | bytes 1048576 | tf_op jit(solution)/shard_map/ppermute | solution.py:150
  75.2 1.8 %pad_maximum_fusion = bf16[128,4096]{0,1:T(8,128)(2,1)S(1)} fusion(bf16[64,4096]{0,1:T(8,128)(2,1)} %copy.24, bf16[64,4096]{0,1:T(8,128)(2,1)S(1)} %copy.23), kind=kLoop, calls=%fused_computation | loop fusion | flops 2097152 | bytes 2097152 | tf_op jit(solution)/shard_map/concatenate | solution.py:153
  77.1 1.6 %copy.25 = bf16[128,64,64]{0,2,1:T(8,128)(2,1)} copy(bf16[128,64,64]{0,1,2:T(8,128)(2,1)S(1)} %bitcast.8) | data formatting | bytes 2097152 | tf_op jit(solution)/shard_map/transpose | solution.py:187
  78.7 1.5 %copy.26.bank_ref = bf16[128,4096]{1,0:T(8,128)(2,1)S(1)} copy(bf16[128,4096]{0,1:T(8,128)(2,1)} %bitcast.9) | data formatting | bytes 2097152 | tf_op jit(solution)/shard_map/reshape | solution.py:187
  80.2 0.0 copy-start.2
  80.2 0.0 collective-permute-done
  80.2 1.4 %broadcast_select_fusion.part_ref = bf16[512,1024]{1,0:T(8,128)(2,1)S(1)} fusion(bf16[512,1024]{1,0:T(8,128)(2,1)} %collective-permute-done, bf16[512,1024]{1,0:T(8,128)(2,1)} %collective-permute-done.1, pred[]{:T(512)S(6)} %or.3), kind=kLoop, calls=%fused_computation.1 | loop fusion | flops 524288 | bytes 3145729 | tf_op jit(solution)/shard_map/jit(_where)/select_n | solution.py:170
  81.7 0.0 copy-start.3
  81.7 0.0 collective-permute-done.2.refs_1_
  81.7 15.5 %collective-permute-done.3.refs_2_ = bf16[512,1024]{1,0:T(8,128)(2,1)} collective-permute-done((bf16[512,1024]{1,0:T(8,128)(2,1)}, bf16[512,1024]{1,0:T(8,128)(2,1)}, u32[]{:S(2)}, u32[]{:S(2)}) %collective-permute-start.3) | collective-permute-done | bytes 1048608 | tf_op jit(solution)/shard_map/ppermute | solution.py:164
  97.2 0.0 copy-done.2
  97.2 17.1 %shard_map.109.total_ref = f32[512,3584]{1,0:T(8,128)S(1)} custom-call(s32[3]{0:T(128)S(1)} %pad_add_fusion.place_ref, bf16[512,1024]{1,0:T(8,128)(2,1)S(1)} %copy-done.2, bf16[512,1024]{1,0:T(8,128)(2,1)} %collective-permute-done.2.refs_1_, bf16[512,1024]{1,0:T(8,128)(2,1)} %collective-permute-done.3.refs_2_, bf16[3584,4096]{1,0:T(8,128)(2,1)} %weight_ref.1, ...), custom_call_target="tpu_custom_call" | custom-call | flops 11274289152 | bytes 32505856 | tf_op jit(solution)/shard_map/pallas_call | solution.py:44
  114.2 12.4 %shard_map.110 = f32[4,256]{1,0:T(4,128)S(1)} custom-call(s32[1]{0:T(128)} %dynamic_slice.6.place_ref, bf16[512,1024]{1,0:T(8,128)(2,1)S(1)} %broadcast_select_fusion.part_ref, bf16[3584,4096]{1,0:T(8,128)(2,1)} %weight_ref.1, f32[512,3584]{1,0:T(8,128)S(1)} %shard_map.109.total_ref, bf16[512,3584]{1,0:T(8,128)(2,1)S(1)} %copy-done.1, ...), custom_call_target="tpu_custom_call" | custom-call | flops 3758096384 | bytes 19398656 | tf_op jit(solution)/shard_map/pallas_call | solution.py:112
  126.6 0.0 collective-permute-start.7
  126.7 1.2 collective-permute-done.7
  127.8 3.0 %collective-permute-start.8 = (f32[4,256]{1,0:T(4,128)S(1)}, f32[4,256]{1,0:T(4,128)S(1)}, u32[]{:S(2)}, u32[]{:S(2)}) collective-permute-start(f32[4,256]{1,0:T(4,128)S(1)} %add.44), channel_id=1, source_target_pairs={{0,4},{4,0},{8,12},{12,8},{1,5},{5,1},{9,13},{13,9},{2,6},{6,2},{1... | collective-permute-start | bytes 12296 | tf_op jit(solution)/shard_map/ppermute | solution.py:22
  130.9 1.6 %collective-permute-done.8 = f32[4,256]{1,0:T(4,128)S(1)} collective-permute-done((f32[4,256]{1,0:T(4,128)S(1)}, f32[4,256]{1,0:T(4,128)S(1)}, u32[]{:S(2)}, u32[]{:S(2)}) %collective-permute-start.8) | collective-permute-done | bytes 4128 | tf_op jit(solution)/shard_map/ppermute | solution.py:22
  132.4 1.7 %collective-permute-start.9 = (f32[4,256]{1,0:T(4,128)S(1)}, f32[4,256]{1,0:T(4,128)S(1)}, u32[]{:S(2)}, u32[]{:S(2)}) collective-permute-start(f32[4,256]{1,0:T(4,128)S(1)} %add.45), channel_id=1, source_target_pairs={{0,8},{4,12},{8,0},{12,4},{1,9},{5,13},{9,1},{13,5},{2,10},{6,14},... | collective-permute-start | bytes 12296 | tf_op jit(solution)/shard_map/ppermute | solution.py:22
  134.2 2.8 %collective-permute-done.9 = f32[4,256]{1,0:T(4,128)S(1)} collective-permute-done((f32[4,256]{1,0:T(4,128)S(1)}, f32[4,256]{1,0:T(4,128)S(1)}, u32[]{:S(2)}, u32[]{:S(2)}) %collective-permute-start.9) | collective-permute-done | bytes 4128 | tf_op jit(solution)/shard_map/ppermute | solution.py:22
  137.0 0.6 add.46
  (15 shorter events, 0.1 us)
Async XLA Ops:
  0.0 16.6 %copy-start = (bf16[512,1024]{1,0:T(8,128)(2,1)S(1)}, bf16[512,1024]{1,0:T(8,128)(2,1)}, u32[]{:S(2)}) copy-start(bf16[512,1024]{1,0:T(8,128)(2,1)} %param.12) | copy-start | bytes 3145732
  0.0 21.1 %copy-start.8 = (s32[4]{0:T(128)S(1)}, s32[4]{0:T(128)}, u32[]{:S(2)}) copy-start(s32[4]{0:T(128)} %constant.42.clone) | copy-start | bytes 52
  0.0 22.2 %copy-start.6 = (s32[256]{0:T(256)S(1)}, s32[256]{0:T(256)}, u32[]{:S(2)}) copy-start(s32[256]{0:T(256)} %param.19) | copy-start | bytes 3076
  0.0 72.6 %collective-permute-start.1 = (bf16[512,1024]{1,0:T(8,128)(2,1)}, bf16[512,1024]{1,0:T(8,128)(2,1)}, u32[]{:S(2)}, u32[]{:S(2)}) collective-permute-start(bf16[512,1024]{1,0:T(8,128)(2,1)} %refs_0_.1), channel_id=1, source_target_pairs={{4,8},{8,4},{0,0},{12,12},{5,9},{9,5},{1,1},{13,13},{6,10},{10,6},... | collective-permute-start | bytes 3145736 | tf_op jit(solution)/shard_map/ppermute | solution.py:164
  9.6 72.1 %collective-permute-start.2 = (bf16[512,1024]{1,0:T(8,128)(2,1)}, bf16[512,1024]{1,0:T(8,128)(2,1)}, u32[]{:S(2)}, u32[]{:S(2)}) collective-permute-start(bf16[512,1024]{1,0:T(8,128)(2,1)} %refs_0_.1), channel_id=1, source_target_pairs={{0,4},{4,0},{8,12},{12,8},{1,5},{5,1},{9,13},{13,9},{2,6},{6,2},{1... | collective-permute-start | bytes 3145736 | tf_op jit(solution)/shard_map/ppermute | solution.py:164
  9.6 70.6 %collective-permute-start = (bf16[512,1024]{1,0:T(8,128)(2,1)}, bf16[512,1024]{1,0:T(8,128)(2,1)}, u32[]{:S(2)}, u32[]{:S(2)}) collective-permute-start(bf16[512,1024]{1,0:T(8,128)(2,1)} %refs_0_.1), channel_id=1, source_target_pairs={{0,12},{12,0},{1,13},{13,1},{2,14},{14,2},{3,15},{15,3},{16,28},{2... | collective-permute-start | bytes 3145736 | tf_op jit(solution)/shard_map/ppermute | solution.py:164
  17.9 48.3 %copy-start.4 = (bf16[64,4096]{1,0:T(8,128)(2,1)S(1)}, bf16[64,4096]{1,0:T(8,128)(2,1)}, u32[]{:S(2)}) copy-start(bf16[64,4096]{1,0:T(8,128)(2,1)} %param.18) | copy-start | bytes 1572868
  17.9 42.1 %collective-permute-start.4 = (f32[64,512]{1,0:T(8,128)S(1)}, f32[64,512]{1,0:T(8,128)}, u32[]{:S(2)}, u32[]{:S(2)}) collective-permute-start(f32[64,512]{1,0:T(8,128)S(1)} %fusion), channel_id=1, source_target_pairs={{0,4},{4,0},{8,12},{12,8},{1,5},{5,1},{9,13},{13,9},{2,6},{6,2},{1... | collective-permute-start | bytes 393224 | tf_op jit(solution)/shard_map/ppermute | solution.py:22
  18.0 54.9 %collective-permute-start.6 = (bf16[64,4096]{1,0:T(8,128)(2,1)}, bf16[64,4096]{1,0:T(8,128)(2,1)}, u32[]{:S(2)}, u32[]{:S(2)}) collective-permute-start(bf16[64,4096]{1,0:T(8,128)(2,1)} %param.18), channel_id=1, source_target_pairs={{0,2},{2,0},{1,3},{3,1},{4,6},{6,4},{5,7},{7,5},{8,10},{10,8},{9,1... | collective-permute-start | bytes 1572872 | tf_op jit(solution)/shard_map/ppermute | solution.py:150
  21.0 45.8 %copy-start.7 = (s32[4]{0:T(128)S(1)}, s32[4]{0:T(128)}, u32[]{:S(2)}) copy-start(s32[4]{0:T(128)} %constant.43.clone) | copy-start | bytes 52
  21.0 46.4 %copy-start.5 = (s32[1,512]{1,0:T(1,128)S(1)}, s32[1,512]{1,0:T(1,128)}, u32[]{:S(2)}) copy-start(s32[1,512]{1,0:T(1,128)} %param.17) | copy-start | bytes 6148
  61.6 10.0 %collective-permute-start.5 = (f32[64,512]{1,0:T(8,128)}, f32[64,512]{1,0:T(8,128)}, u32[]{:S(2)}, u32[]{:S(2)}) collective-permute-start(f32[64,512]{1,0:T(8,128)} %add.37), channel_id=1, source_target_pairs={{0,8},{4,12},{8,0},{12,4},{1,9},{5,13},{9,1},{13,5},{2,10},{6,14},... | collective-permute-start | bytes 393224 | tf_op jit(solution)/shard_map/ppermute | solution.py:22
  72.6 24.5 %collective-permute-start.3 = (bf16[512,1024]{1,0:T(8,128)(2,1)}, bf16[512,1024]{1,0:T(8,128)(2,1)}, u32[]{:S(2)}, u32[]{:S(2)}) collective-permute-start(bf16[512,1024]{1,0:T(8,128)(2,1)} %collective-permute-done.1), channel_id=1, source_target_pairs={{0,8},{8,12},{12,4},{4,0},{1,9},{9,13},{13,5},{5,1},{2,10},{10,14}... | collective-permute-start | bytes 3145736 | tf_op jit(solution)/shard_map/ppermute | solution.py:164
  80.2 17.0 %copy-start.2 = (bf16[512,1024]{1,0:T(8,128)(2,1)S(1)}, bf16[512,1024]{1,0:T(8,128)(2,1)}, u32[]{:S(2)}) copy-start(bf16[512,1024]{1,0:T(8,128)(2,1)} %refs_0_.1) | copy-start | bytes 3145732
  81.7 32.6 %copy-start.3 = (f32[128,256]{1,0:T(8,128)S(1)}, f32[128,256]{1,0:T(8,128)}, u32[]{:S(2)}) copy-start(f32[128,256]{1,0:T(8,128)} %compare_convert_fusion.pick_ref) | copy-start | bytes 393220
  97.2 17.1 %copy-start.1 = (bf16[512,3584]{1,0:T(8,128)(2,1)S(1)}, bf16[512,3584]{1,0:T(8,128)(2,1)}, u32[]{:S(2)}) copy-start(bf16[512,3584]{1,0:T(8,128)(2,1)} %gate_ref.1) | copy-start | bytes 11010052
  126.6 1.2 collective-permute-start.7
  127.8 4.6 %collective-permute-start.8 = (f32[4,256]{1,0:T(4,128)S(1)}, f32[4,256]{1,0:T(4,128)S(1)}, u32[]{:S(2)}, u32[]{:S(2)}) collective-permute-start(f32[4,256]{1,0:T(4,128)S(1)} %add.44), channel_id=1, source_target_pairs={{0,4},{4,0},{8,12},{12,8},{1,5},{5,1},{9,13},{13,9},{2,6},{6,2},{1... | collective-permute-start | bytes 12296 | tf_op jit(solution)/shard_map/ppermute | solution.py:22
  132.4 4.5 %collective-permute-start.9 = (f32[4,256]{1,0:T(4,128)S(1)}, f32[4,256]{1,0:T(4,128)S(1)}, u32[]{:S(2)}, u32[]{:S(2)}) collective-permute-start(f32[4,256]{1,0:T(4,128)S(1)} %add.45), channel_id=1, source_target_pairs={{0,8},{4,12},{8,0},{12,4},{1,9},{5,13},{9,1},{13,5},{2,10},{6,14},... | collective-permute-start | bytes 12296 | tf_op jit(solution)/shard_map/ppermute | solution.py:22

commit v2 on v0

v2 whole, which is shorter than its diff:
```python
import functools

import jax
import jax.numpy as jnp
from jax import lax
from jax.experimental import pallas as pl
from jax.experimental.pallas import tpu as pltpu
from jax.sharding import PartitionSpec as P

EX_DEV = 4
TILE = 512
EXACT = lax.Precision.HIGHEST


def after(value, *deps):
    return lax.optimization_barrier((value, *deps))[0]


def sum_over(value, axis, size):
    step = 1
    while step < size:
        value = value + lax.ppermute(value, axis, [(i, i ^ step) for i in range(size)])
        step *= 2
    return value


def tile_of(count):
    return max((t for t in range(128, TILE + 1, 128) if count % t == 0), default=count)


def two_terms(value):
    high = value.astype(jnp.bfloat16)
    return high, (value - high.astype(jnp.float32)).astype(jnp.bfloat16)


IN_VMEM = pl.BlockSpec(memory_space=pltpu.VMEM)
IN_SMEM = pl.BlockSpec(memory_space=pltpu.SMEM)
ANYWHERE = pl.BlockSpec(memory_space=pl.ANY)


def column_copy(weight_ref, place, held_ref, sem_ref, chunk):
    hidden, width = held_ref.shape
    tile = tile_of(hidden)
    rows = pl.ds(pl.multiple_of(chunk * tile, tile), tile)
    return pltpu.make_async_copy(
        weight_ref.at[rows, pl.ds(pl.multiple_of(place * width, width), width)],
        held_ref.at[rows, :],
        sem_ref.at[chunk],
    )


def chunks_of(held_ref):
    return held_ref.shape[0] // tile_of(held_ref.shape[0])


def rows_of(held_ref, chunk):
    tile = tile_of(held_ref.shape[0])
    return pl.ds(pl.multiple_of(chunk * tile, tile), tile)


def hidden_kernel(blocks, has_base, places_ref, weight_ref, *refs):
    parts, refs = refs[:blocks], refs[blocks:]
    base_ref, refs = (refs[0], refs[1:]) if has_base else (None, refs)
    total_ref, mark_ref, kept_ref, refs = refs[0], refs[1], refs[2], refs[3:]
    held, turned, sems, kept_sem = refs[:blocks], refs[blocks : 2 * blocks], refs[2 * blocks : -1], refs[-1]
    chunks = chunks_of(total_ref)

    @pl.loop(0, chunks)
    def _(chunk):
        for k in range(blocks):
            column_copy(weight_ref, places_ref[k], held[k], sems[k], chunk).start()

    @pl.loop(0, chunks if has_base else 0)
    def _(chunk):
        column_copy(weight_ref, places_ref[blocks], kept_ref, kept_sem, chunk).start()

    for part, turn in zip(parts, turned):
        turn[...] = part[...].T
    mark_ref[...] = jnp.zeros_like(mark_ref)

    @pl.loop(0, chunks)
    def _(chunk):
        rows = rows_of(total_ref, chunk)
        total = base_ref[rows, :] if has_base else 0.0
        for k in range(blocks):
            column_copy(weight_ref, places_ref[k], held[k], sems[k], chunk).wait()
            total += jnp.dot(held[k][rows, :], turned[k][...], preferred_element_type=jnp.float32)
        total_ref[rows, :] = total

    @pl.loop(0, chunks if has_base else 0)
    def _(chunk):
        column_copy(weight_ref, places_ref[blocks], kept_ref, kept_sem, chunk).wait()


def held_in_vmem(value):
    return pltpu.with_memory_space_constraint(value, pltpu.VMEM)


def hidden_sum(parts, places, weight, base=None):
    tokens, width = parts[0].shape
    hidden = weight.shape[0]
    blocks = len(parts)
    bases = [] if base is None else [held_in_vmem(base)]
    kept = (hidden, width) if bases else (8, 128)
    chunks = pltpu.SemaphoreType.DMA((hidden // tile_of(hidden),))
    return pl.pallas_call(
        functools.partial(hidden_kernel, blocks, bool(bases)),
        in_specs=[IN_SMEM, ANYWHERE] + [IN_VMEM] * (blocks + len(bases)),
        out_specs=[IN_VMEM] * 3,
        scratch_shapes=[pltpu.VMEM((hidden, width), weight.dtype)] * blocks
        + [pltpu.VMEM((width, tokens), parts[0].dtype)] * blocks
        + [chunks] * (blocks + 1),
        out_shape=[
            pltpu.VMEM((hidden, tokens), jnp.float32),
            jax.ShapeDtypeStruct((8, 128), jnp.float32),
            pltpu.VMEM(kept, weight.dtype),
        ],
        input_output_aliases={2 + blocks: 0} if bases else {},
        compiler_params=pltpu.CompilerParams(vmem_limit_bytes=(6 + 9 * blocks) << 20),
        cost_estimate=pl.CostEstimate(
            flops=2 * blocks * tokens * width * hidden,
            bytes_accessed=2 * blocks * width * (tokens + hidden),
            transcendentals=0,
        ),
    )(places, weight, *parts, *bases)


def silu(gate):
    gate = gate.astype(jnp.float32)
    return gate / (1.0 + jnp.exp(-gate))


def factor_kernel(gate_ref, factor_ref):
    @pl.loop(0, chunks_of(factor_ref))
    def _(chunk):
        rows = rows_of(factor_ref, chunk)
        factor_ref[rows, :] = silu(gate_ref[:, rows]).T


def factors(gate):
    tokens, hidden = gate.shape
    return pl.pallas_call(
        factor_kernel,
        in_specs=[IN_VMEM],
        out_specs=IN_VMEM,
        out_shape=pltpu.VMEM((hidden, tokens), jnp.float32),
        compiler_params=pltpu.CompilerParams(vmem_limit_bytes=16 << 20),
        cost_estimate=pl.CostEstimate(
            flops=8 * tokens * hidden, bytes_accessed=6 * tokens * hidden, transcendentals=tokens * hidden
        ),
    )(gate)


def term_loop(part_ref, held_ref, total_ref, factor_ref, proj_ref, out_ref, turned, ahead):
    columns = slice(ahead, ahead + part_ref.shape[0])
    turned[...] = part_ref[...].T
    out_ref[...] = jnp.zeros_like(out_ref)

    @pl.loop(0, chunks_of(held_ref))
    def _(chunk):
        rows = rows_of(held_ref, chunk)
        hidden = total_ref[rows, columns] + jnp.dot(
            held_ref[rows, :], turned[...], preferred_element_type=jnp.float32
        )
        up = (hidden * factor_ref[rows, columns]).astype(jnp.bfloat16)
        out_ref[...] += jnp.dot(proj_ref[:, rows], up, preferred_element_type=jnp.float32)


def first_kernel(part_ref, held_ref, total_ref, factor_ref, proj_ref, out_ref, turned):
    term_loop(part_ref, held_ref, total_ref, factor_ref, proj_ref, out_ref, turned, 0)


def first_terms(part, held, total, factor, proj):
    tokens, width = part.shape
    return pl.pallas_call(
        first_kernel,
        in_specs=[IN_VMEM] * 5,
        out_specs=IN_VMEM,
        scratch_shapes=[pltpu.VMEM((width, tokens), part.dtype)],
        out_shape=pltpu.VMEM((proj.shape[0], tokens), jnp.float32),
        compiler_params=pltpu.CompilerParams(vmem_limit_bytes=12 << 20),
        cost_estimate=pl.CostEstimate(
            flops=2 * tokens * width * held.shape[0], bytes_accessed=2 * tokens * width, transcendentals=0
        ),
    )(part, held_in_vmem(held), held_in_vmem(total), held_in_vmem(factor), proj)


def last_kernel(
    scale, part_ref, held_ref, total_ref, factor_ref, proj_ref, first_ref, inside_ref, bank_ref, scores_ref,
    turned, out_ref, rows_ref, flat_ref, pairs_ref,
):
    tokens = part_ref.shape[0]
    ahead = first_ref.shape[1]
    term_loop(part_ref, held_ref, total_ref, factor_ref, proj_ref, out_ref, turned, ahead)
    width = out_ref.shape[0]
    for ref, columns in ((first_ref, slice(0, ahead)), (out_ref, slice(ahead, ahead + tokens))):
        high, low = two_terms(ref[...])
        rows_ref[:width, columns] = high
        rows_ref[width:, columns] = low
    sketch = jnp.dot(rows_ref[...], inside_ref[0], preferred_element_type=jnp.float32)
    sketch = sketch[:width] + sketch[width:]
    sketch += jnp.dot(rows_ref[:width], inside_ref[1], preferred_element_type=jnp.float32)
    for n in range(0, EX_DEV, 2):
        pairs_ref[n // 2 * width : (n // 2 + 1) * width] = sketch[:, n * width : (n + 2) * width]
    half = width // 2
    left = lax.broadcasted_iota(jnp.int32, (half, 2 * width), 1) < width
    for n in range(0, EX_DEV, 2):
        even = pairs_ref[pl.ds(n * half, half, stride=2), :]
        odd = pairs_ref[pl.ds(n * half + 1, half, stride=2), :]
        flat_ref[n * half : (n + 1) * half] = jnp.where(left, even, pltpu.roll(odd, width, 1))
        flat_ref[(n + 1) * half : (n + 2) * half] = jnp.where(left, pltpu.roll(even, width, 1), odd)
    flat = jnp.concatenate([flat_ref[pl.ds(p, EX_DEV, stride=half), :] for p in range(half)], axis=1)
    bank = bank_ref[...]
    found = sum(jnp.dot(t, bank, preferred_element_type=jnp.float32) for t in two_terms(flat))
    scores_ref[...] = scale * found


def last_scores(part, held, total, factor, proj, first, inside, bank, scale):
    tokens, width = part.shape
    hidden = held.shape[0]
    factors = proj.shape[0]
    return pl.pallas_call(
        functools.partial(last_kernel, scale),
        in_specs=[IN_VMEM] * 8,
        out_specs=IN_VMEM,
        scratch_shapes=[
            pltpu.VMEM((width, tokens), part.dtype),
            pltpu.VMEM((factors, tokens), jnp.float32),
            pltpu.VMEM((2 * factors, inside.shape[1]), jnp.bfloat16),
            pltpu.VMEM((EX_DEV * factors // 2, 2 * factors), jnp.float32),
            pltpu.VMEM((EX_DEV // 2 * factors, 2 * factors), jnp.float32),
        ],
        out_shape=jax.ShapeDtypeStruct((EX_DEV, bank.shape[1]), jnp.float32),
        compiler_params=pltpu.CompilerParams(vmem_limit_bytes=14 << 20),
        cost_estimate=pl.CostEstimate(
            flops=2 * tokens * width * hidden, bytes_accessed=2 * tokens * width, transcendentals=0
        ),
    )(part, *map(held_in_vmem, (held, total, factor)), proj, *map(held_in_vmem, (first, inside, bank)))


def spread_kernel(seg_ref, *refs):
    inside_ref = refs[-1]
    rows = sum(ref[...] for ref in refs[:-1])
    for n in range(EX_DEV):
        columns = slice(n * rows.shape[0], (n + 1) * rows.shape[0])
        high, low = two_terms(jnp.where(seg_ref[...] == n, rows, 0.0).T)
        inside_ref[0, :, columns] = high
        inside_ref[1, :, columns] = low


def spread(segments, *terms):
    width, tokens = terms[0].shape
    return pl.pallas_call(
        spread_kernel,
        out_shape=jax.ShapeDtypeStruct((2, tokens, EX_DEV * width), jnp.bfloat16),
        compiler_params=pltpu.CompilerParams(vmem_limit_bytes=8 << 20),
    )(segments, *terms)


def bank_parts(query_bank, size):
    return [query_bank] + [
        lax.ppermute(query_bank, "dp", [(i, (i + k) % size) for i in range(size)]) for k in range(1, size)
    ]


def picked(parts, query_ids):
    size, held = len(parts), parts[0].shape[0]
    me = lax.axis_index("dp")
    rows = jnp.arange(held, dtype=jnp.int32)
    places = jnp.concatenate([(me - k) % size * held + rows for k in range(size)])
    pick = (places[:, None] == query_ids[None, :]).astype(jnp.bfloat16)
    return lax.dot_general(
        jnp.concatenate(parts), pick, (((0,), (0,)), ((), ())), preferred_element_type=jnp.float32
    ).astype(jnp.bfloat16)


def body(
    sizes, out_grad, layer_in, gate_pre, down_weight, proj_in, proj_out, segment_ids, query_bank, query_ids
):
    tensor = sizes["tensor"]
    me = lax.axis_index("tensor")
    scale = 1.0 / (8.0 * proj_in.shape[1])
    proj = proj_out.T

    send = lambda value, pairs: lax.ppermute(value, "tensor", pairs)
    pick_of = lambda *t: jnp.asarray(t, jnp.int32)[me][None]
    project = lambda rows: lax.dot_general(
        proj_in, rows, (((0,), (1,)), ((), ())), preferred_element_type=jnp.float32
    )

    half = out_grad.shape[0] // 2
    in_part = project(layer_in)
    if tensor == 4:
        pairs, crossed, onward = [(0, 1), (1, 0), (2, 3), (3, 2)], [(0, 3), (3, 0)], [(0, 2), (2, 3), (3, 1), (1, 0)]
        in_near = send(in_part, pairs)
        middle = send(out_grad, [(1, 2), (2, 1), (0, 0), (3, 3)])
        near = send(out_grad, pairs)
        here = after(out_grad, in_part)
        cross = send(here, crossed)
        factor = factors(after(gate_pre, in_part))
        middle = after(middle, factor)
        halves = [middle[:half], middle[half:]]
        in_sum = in_part + after((in_near, in_part), *halves)[0]
        in_rest = send(in_sum, crossed + [(1, 2), (2, 1)])
        far = [send(rows, onward) for rows in halves]
        near, query_bank = after((near, query_bank), in_sum)
        parts = bank_parts(query_bank, sizes["dp"])
        total, mark, _ = hidden_sum([here, near], jnp.concatenate([me[None], me[None] ^ 1]), down_weight)
        bank = picked(after(parts, mark), query_ids)
        cross = after(cross, bank)
        rest = jnp.where((me == 0) | (me == 3), cross, middle)
        places = jnp.concatenate([pick_of(3, 2, 1, 0), pick_of(2, 3, 0, 1)])
        total, mark, held = hidden_sum([rest], places, down_weight, total)
        far[0] = after(far[0], mark)
    else:
        in_sum, in_rest = sum_over(in_part, "tensor", tensor), jnp.zeros_like(in_part)
        factor = factors(gate_pre)
        gathered = lax.all_gather(out_grad, "tensor", axis=1, tiled=True)
        step = gathered.shape[1] // 4
        blocks = [gathered[:, k * step : (k + 1) * step] for k in range(4)]
        far = [blocks[3][:half], blocks[3][half:]]
        places = jnp.arange(4, dtype=jnp.int32)
        total, _, _ = hidden_sum(blocks[:2], places[:2], down_weight)
        total, _, held = hidden_sum(blocks[2:3], places[2:], down_weight, total)
        bank = picked(bank_parts(query_bank, sizes["dp"]), query_ids)

    first = first_terms(far[0], held, total, factor, proj)
    inside = spread(segment_ids, in_sum, after(in_rest, first))
    scores = last_scores(far[1], held, total, factor, proj, first, inside, bank, scale)
    scores = sum_over(scores, "seq", sizes["seq"])
    return sum_over(scores, "tensor", tensor)


def solution(mesh):
    in_specs = (
        P(("groups", "dp", "seq"), "tensor"),
        P(("groups", "dp", "seq"), "tensor"),
        P(("groups", "dp", "seq"), "tensor"),
        P("tensor", None),
        P("tensor", None),
        P("tensor", None),
        P(("groups", "dp"), "seq"),
        P(("groups", "dp"), None),
        P("groups"),
    )
    out_specs = P(("groups", "dp"), None)
    sizes = {name: mesh.shape[name] for name in mesh.axis_names}
    return jax.shard_map(
        functools.partial(body, sizes), mesh=mesh, in_specs=in_specs, out_specs=out_specs, check_vma=False
    )
```

time: 184 us -> 99.5 us (0.54)
  waiting for transfers between devices: 135 us -> 25.5 us
  Pallas kernels: 0 us -> 33.5 us
  starting transfers between devices: 0.13 us -> 30.9 us
  matrix products: 30.8 us -> 2.12 us
  between operations: 14.6 us -> 0.18 us
  local copies, waits for them, and re-layouts: 2.12 us -> 4.72 us
    all_gather x2 -> x0, waiting for transfers between devices: 83.3 us -> none  [the longest x1 83.3 us: body(): lax.all_gather(out_grad, 'tensor', axis=1, tiled=True)]
    psum x2 -> x0, waiting for transfers between devices: 50.9 us -> none  [the longest x1 33.3 us: body(): summed = lax.psum(stacked, 'tensor')]
    pallas_call x0 -> x6, Pallas kernels: none -> 33.5 us  [the longest x2 19.6 us: hidden_sum(): pl.pallas_call(functools.partial(hidden_kernel, blocks, bool(bases)), in_...]
    ppermute x0 -> x11, starting transfers between devices: none -> 30.9 us  [the longest x7 23.7 us: body(): send = lambda value, pairs: lax.ppermute(value, 'tensor', pairs)]
    dot_general x5 -> x2, matrix products: 30.8 us -> 2.12 us  [the longest x1 1.34 us: body(): lax.dot_general(proj_in, rows, (((0,), (1,)), ((), ())), preferred_elemen...]
    ppermute x0 -> x11, waiting for transfers between devices: none -> 25.5 us  [the longest x7 20.8 us: body(): send = lambda value, pairs: lax.ppermute(value, 'tensor', pairs)]
    dynamic_slice x0 -> x2, local copies, waits for them, and re-layouts: none -> 2.58 us  [body(): pick_of = lambda *t: jnp.asarray(t, jnp.int32)[me][None]]
  transfers between devices with their start and end apart: 4 -> 11, of which waited for: 3 -> 7; matrix products, arithmetic and copies ran while one was open for 2% -> 6% of each run, Pallas kernels for 0% -> 28%
where the time goes in v2:
time: 99.5 us; the launch traced here: 99.2 us
  Pallas kernels  33.5 us (34%)
  starting transfers between devices  30.9 us (31%)
  waiting for transfers between devices  25.5 us (26%)
  local copies, waits for them, and re-layouts  4.72 us (5%)
  other arithmetic  2.21 us (2%)
  matrix products  2.12 us (2%)
    ppermute x7, starting transfers between devices, body(): send = lambda value, pairs: lax.ppermute(value, 'tensor', pairs)  23.7 us
    ppermute x7, waiting for transfers between devices, body(): send = lambda value, pairs: lax.ppermute(value, 'tensor', pairs)  20.8 us
    pallas_call x2, Pallas kernels, hidden_sum(): pl.pallas_call(functools.partial(hidden_kernel, blocks, bool(bases)), in_...  19.6 us
    pallas_call x1, Pallas kernels, last_scores(): pl.pallas_call(functools.partial(last_kernel, scale), in_specs=[IN_VMEM]...  5.9 us
    ppermute x3, starting transfers between devices, sum_over(): lax.ppermute(value, axis, [(i, i ^ step) for i in range(size)])  5.73 us
    pallas_call x1, Pallas kernels, first_terms(): pl.pallas_call(first_kernel, in_specs=[IN_VMEM] * 5, out_specs=IN_VMEM, s...  4.89 us
    ppermute x3, waiting for transfers between devices, sum_over(): lax.ppermute(value, axis, [(i, i ^ step) for i in range(size)])  4.8 us
    dynamic_slice x2, local copies, waits for them, and re-layouts, body(): pick_of = lambda *t: jnp.asarray(t, jnp.int32)[me][None]  2.58 us
  transfers between devices with their start and end apart: 11, of which 7 were waited for; matrix products, arithmetic and copies ran while one was open for 6% of the time, Pallas kernels for 28%

profile of v2, /device:TPU:0, one launch (start us, length us, event | category | flops | bytes accessed | tf_op | source)
XLA Modules:
  0.0 99.2 jit_solution(3602435736962926578)
XLA Ops:
  0.0 0.0 copy-start
  0.0 2.0 %collective-permute-start = (bf16[512,1024]{1,0:T(8,128)(2,1)}, bf16[512,1024]{1,0:T(8,128)(2,1)S(1)}, u32[]{:S(2)}, u32[]{:S(2)}) collective-permute-start(bf16[512,1024]{1,0:T(8,128)(2,1)} %refs_0_), channel_id=1, source_target_pairs={{4,8},{8,4},{0,0},{12,12},{5,9},{9,5},{1,1},{13,13},{6,10},{10,6},... | collective-permute-start | bytes 3145736 | tf_op jit(solution)/shard_map/ppermute | solution.py:285
  2.0 4.7 %collective-permute-start.3 = (bf16[512,1024]{1,0:T(8,128)(2,1)}, bf16[512,1024]{1,0:T(8,128)(2,1)S(1)}, u32[]{:S(2)}, u32[]{:S(2)}) collective-permute-start(bf16[512,1024]{1,0:T(8,128)(2,1)} %refs_0_), channel_id=1, source_target_pairs={{0,4},{4,0},{8,12},{12,8},{1,5},{5,1},{9,13},{13,9},{2,6},{6,2},{1... | collective-permute-start | bytes 3145736 | tf_op jit(solution)/shard_map/ppermute | solution.py:285
  6.7 0.0 copy-done
  6.7 1.3 %fusion.8 = f32[64,512]{1,0:T(8,128)S(1)} fusion(bf16[1024,64]{0,1:T(8,128)(2,1)} %param.15, bf16[512,1024]{1,0:T(8,128)(2,1)S(1)} %copy-done), kind=kOutput, calls=%fused_computation.15 | convolution fusion | flops 67108864 | bytes 1310720 | tf_op jit(solution)/shard_map/dot_general | solution.py:287
  8.1 0.1 collective-permute-start.4
  8.1 4.3 %collective-permute-start.2 = (bf16[512,1024]{1,0:T(8,128)(2,1)}, bf16[512,1024]{1,0:T(8,128)(2,1)S(1)}, u32[]{:S(2)}, u32[]{:S(2)}) collective-permute-start(bf16[512,1024]{1,0:T(8,128)(2,1)} %refs_0_), channel_id=1, source_target_pairs={{0,12},{12,0},{1,13},{13,1},{2,14},{14,2},{3,15},{15,3},{16,28},{2... | collective-permute-start | bytes 3145736 | tf_op jit(solution)/shard_map/ppermute | solution.py:285
  12.4 1.3 %dynamic_slice.6 = s32[1]{0:T(128)} dynamic-slice(s32[4]{0:T(128)} %constant.42.clone, s32[]{:T(128)S(6)} %select_n.23), dynamic_slice_sizes={1} | dynamic-slice | bytes 12 | tf_op jit(solution)/shard_map/dynamic_slice | solution.py:286
  13.7 1.3 %dynamic_slice.7 = s32[1]{0:T(128)} dynamic-slice(s32[4]{0:T(128)} %constant.43.clone, s32[]{:T(128)S(6)} %select_n.23), dynamic_slice_sizes={1} | dynamic-slice | bytes 12 | tf_op jit(solution)/shard_map/dynamic_slice | solution.py:286
  15.0 2.0 %copy-done.2 = bf16[512,3584]{1,0:T(8,128)(2,1)S(1)} copy-done((bf16[512,3584]{1,0:T(8,128)(2,1)S(1)}, bf16[512,3584]{1,0:T(8,128)(2,1)}, u32[]{:S(2)}) %copy-start.2) | copy-done | bytes 3670040
  17.1 2.5 %shard_map.109.factor_ref = f32[3584,512]{1,0:T(8,128)S(1)} custom-call(bf16[512,3584]{1,0:T(8,128)(2,1)S(1)} %copy-done.2), custom_call_target="tpu_custom_call" | custom-call | flops 14680064 | bytes 11010048 | tf_op jit(solution)/shard_map/pallas_call | solution.py:142
  19.6 0.1 pad_add_fusion.2.places_ref
  19.6 0.1 pad_add_fusion.1
  19.7 1.3 %pad_add_fusion.places_ref = s32[2]{0:T(128)S(1)} fusion(s32[1]{0:T(128)} %dynamic_slice.7, s32[1]{0:T(128)} %dynamic_slice.6), kind=kLoop, calls=%fused_computation.8 | loop fusion | flops 2 | bytes 16 | tf_op jit(solution)/shard_map/concatenate | solution.py:312
  21.0 0.0 collective-permute-done
  21.0 0.1 fusion.7
  21.1 10.2 %collective-permute-start.6 = (bf16[256,1024]{1,0:T(8,128)(2,1)S(1)}, bf16[256,1024]{1,0:T(8,128)(2,1)S(1)}, u32[]{:S(2)}, u32[]{:S(2)}) collective-permute-start(bf16[256,1024]{1,0:T(8,128)(2,1)S(1)} %get-tuple-element.31), channel_id=1, source_target_pairs={{0,8},{8,12},{12,4},{4,0},{1,9},{9,13},{13,5},{5,1},{2,10},{10,14}... | collective-permute-start | bytes 1572872 | tf_op jit(solution)/shard_map/ppermute | solution.py:285
  31.3 0.1 collective-permute-start.1
  31.4 3.9 %collective-permute-done.4 = f32[64,512]{1,0:T(8,128)S(1)} collective-permute-done((f32[64,512]{1,0:T(8,128)S(1)}, f32[64,512]{1,0:T(8,128)S(1)}, u32[]{:S(2)}, u32[]{:S(2)}) %collective-permute-start.4) | collective-permute-done | bytes 131104 | tf_op jit(solution)/shard_map/ppermute | solution.py:285
  35.3 0.0 copy-start.7
  35.3 2.4 %collective-permute-start.7 = (f32[64,512]{1,0:T(8,128)S(1)}, f32[64,512]{1,0:T(8,128)S(1)}, u32[]{:S(2)}, u32[]{:S(2)}) collective-permute-start(f32[64,512]{1,0:T(8,128)S(1)} %add.37.refs_0_), channel_id=1, source_target_pairs={{0,12},{12,0},{4,8},{8,4},{1,13},{13,1},{5,9},{9,5},{2,14},{14,2},... | collective-permute-start | bytes 393224 | tf_op jit(solution)/shard_map/ppermute | solution.py:285
  37.7 0.0 collective-permute-done.3.refs_1_
  37.7 0.0 copy-done.6
  37.7 1.5 %collective-permute-start.5 = (bf16[64,4096]{1,0:T(8,128)(2,1)S(1)}, bf16[64,4096]{1,0:T(8,128)(2,1)S(1)}, u32[]{:S(2)}, u32[]{:S(2)}) collective-permute-start(bf16[64,4096]{1,0:T(8,128)(2,1)S(1)} %copy-done.6), channel_id=1, source_target_pairs={{0,2},{2,0},{1,3},{3,1},{4,6},{6,4},{5,7},{7,5},{8,10},{10,8},{9,1... | collective-permute-start | bytes 1572872 | tf_op jit(solution)/shard_map/ppermute | solution.py:262
  39.2 0.0 copy-done.4
  39.2 11.8 %shard_map.110 = (f32[3584,512]{1,0:T(8,128)S(1)}, f32[8,128]{1,0:T(8,128)}, bf16[8,128]{1,0:T(8,128)(2,1)}) custom-call(s32[2]{0:T(128)S(1)} %pad_add_fusion.2.places_ref, bf16[3584,4096]{1,0:T(8,128)(2,1)} %weight_ref.3, bf16[512,1024]{1,0:T(8,128)(2,1)S(1)} %copy-done.4, bf16[512,1024]{1,0:T(8,128)(2,1)S(1)} %collective-permute-done.3.refs_1_), custom_call_target="tpu_custom_call" | custom-call | flops 7516192768 | bytes 16777216 | tf_op jit(solution)/shard_map/pallas_call | solution.py:106
  51.0 0.0 collective-permute-done.5
  51.0 0.8 convolution_convert_fusion.bank_ref
  51.8 5.9 %collective-permute-done.2 = bf16[512,1024]{1,0:T(8,128)(2,1)S(1)} collective-permute-done((bf16[512,1024]{1,0:T(8,128)(2,1)}, bf16[512,1024]{1,0:T(8,128)(2,1)S(1)}, u32[]{:S(2)}, u32[]{:S(2)}) %collective-permute-start.2) | collective-permute-done | bytes 1048608 | tf_op jit(solution)/shard_map/ppermute | solution.py:285
  57.7 0.1 broadcast_select_fusion.refs_0_
  57.8 9.6 %collective-permute-done.6.part_ref = bf16[256,1024]{1,0:T(8,128)(2,1)S(1)} collective-permute-done((bf16[256,1024]{1,0:T(8,128)(2,1)S(1)}, bf16[256,1024]{1,0:T(8,128)(2,1)S(1)}, u32[]{:S(2)}, u32[]{:S(2)}) %collective-permute-start.6) | collective-permute-done | bytes 524320 | tf_op jit(solution)/shard_map/ppermute | solution.py:285
  67.5 7.9 %shard_map.111 = (f32[3584,512]{1,0:T(8,128)S(1)}, f32[8,128]{1,0:T(8,128)}, bf16[3584,1024]{1,0:T(8,128)(2,1)S(1)}) custom-call(s32[2]{0:T(128)S(1)} %pad_add_fusion.places_ref, bf16[3584,4096]{1,0:T(8,128)(2,1)} %weight_ref.3, bf16[512,1024]{1,0:T(8,128)(2,1)S(1)} %broadcast_select_fusion.refs_0_, ...), custom_call_target="tpu_custom_call", output_to_operand_aliasing={{0}: (3, {})} | custom-call | flops 3758096384 | bytes 8388608 | tf_op jit(solution)/shard_map/pallas_call | solution.py:106
  75.3 0.0 copy-start.5
  75.3 4.9 %shard_map.112.first_ref = f32[64,256]{1,0:T(8,128)S(1)} custom-call(bf16[256,1024]{1,0:T(8,128)(2,1)S(1)} %collective-permute-done.6.part_ref, bf16[3584,1024]{1,0:T(8,128)(2,1)S(1)} %get-tuple-element.28.held_ref, f32[3584,512]{1,0:T(8,128)S(1)} %get-tuple-element.29.total_ref, f32[3584,512]{1,0:T(8,128)S(1)} %shard_map.109.factor_ref, ...), custom_call_target="tpu_custom_call" | custom-call | flops 1879048192 | bytes 524288 | tf_op jit(solution)/shard_map/pallas_call | solution.py:175
  80.2 1.3 %collective-permute-done.7.refs_1_ = f32[64,512]{1,0:T(8,128)S(1)} collective-permute-done((f32[64,512]{1,0:T(8,128)S(1)}, f32[64,512]{1,0:T(8,128)S(1)}, u32[]{:S(2)}, u32[]{:S(2)}) %collective-permute-start.7) | collective-permute-done | bytes 131104 | tf_op jit(solution)/shard_map/ppermute | solution.py:285
  81.5 0.0 copy-done.5
  81.5 0.6 shard_map.113.inside_ref
  82.2 0.0 collective-permute-done.1.part_ref
  82.2 0.0 copy-start.1
  82.2 5.9 %shard_map.114 = f32[4,256]{1,0:T(4,128)S(1)} custom-call(bf16[256,1024]{1,0:T(8,128)(2,1)S(1)} %collective-permute-done.1.part_ref, bf16[3584,1024]{1,0:T(8,128)(2,1)S(1)} %get-tuple-element.28.held_ref, f32[3584,512]{1,0:T(8,128)S(1)} %get-tuple-element.29.total_ref, f32[3584,512]{1,0:T(8,128)S(1)} %shard_map.109.factor_ref, bf16[64,3584]{1,0:T(8,128)(2,1)S(1)} %bitcast.5, ...), custom_call_target="tpu_custom_call" | custom-call | flops 1879048192 | bytes 524288 | tf_op jit(solution)/shard_map/pallas_call | solution.py:222
  88.1 0.0 collective-permute-start.8
  88.1 1.2 %collective-permute-done.8 = f32[4,256]{1,0:T(4,128)S(1)} collective-permute-done((f32[4,256]{1,0:T(4,128)S(1)}, f32[4,256]{1,0:T(4,128)S(1)}, u32[]{:S(2)}, u32[]{:S(2)}) %collective-permute-start.8) | collective-permute-done | bytes 4128 | tf_op jit(solution)/shard_map/ppermute | solution.py:22
  89.3 3.3 %collective-permute-start.9 = (f32[4,256]{1,0:T(4,128)S(1)}, f32[4,256]{1,0:T(4,128)S(1)}, u32[]{:S(2)}, u32[]{:S(2)}) collective-permute-start(f32[4,256]{1,0:T(4,128)S(1)} %add.44), channel_id=1, source_target_pairs={{0,4},{4,0},{8,12},{12,8},{1,5},{5,1},{9,13},{13,9},{2,6},{6,2},{1... | collective-permute-start | bytes 12296 | tf_op jit(solution)/shard_map/ppermute | solution.py:22
  92.5 1.6 %collective-permute-done.9 = f32[4,256]{1,0:T(4,128)S(1)} collective-permute-done((f32[4,256]{1,0:T(4,128)S(1)}, f32[4,256]{1,0:T(4,128)S(1)}, u32[]{:S(2)}, u32[]{:S(2)}) %collective-permute-start.9) | collective-permute-done | bytes 4128 | tf_op jit(solution)/shard_map/ppermute | solution.py:22
  94.1 2.5 %collective-permute-start.10 = (f32[4,256]{1,0:T(4,128)S(1)}, f32[4,256]{1,0:T(4,128)S(1)}, u32[]{:S(2)}, u32[]{:S(2)}) collective-permute-start(f32[4,256]{1,0:T(4,128)S(1)} %add.45), channel_id=1, source_target_pairs={{0,8},{4,12},{8,0},{12,4},{1,9},{5,13},{9,1},{13,5},{2,10},{6,14},... | collective-permute-start | bytes 12296 | tf_op jit(solution)/shard_map/ppermute | solution.py:22
  96.6 2.0 %collective-permute-done.10 = f32[4,256]{1,0:T(4,128)S(1)} collective-permute-done((f32[4,256]{1,0:T(4,128)S(1)}, f32[4,256]{1,0:T(4,128)S(1)}, u32[]{:S(2)}, u32[]{:S(2)}) %collective-permute-start.10) | collective-permute-done | bytes 4128 | tf_op jit(solution)/shard_map/ppermute | solution.py:22
  98.6 0.6 add.46
  99.2 0.0 copy-done.1
  (10 shorter events, 0.0 us)
Async XLA Ops:
  0.0 6.7 %copy-start = (bf16[512,1024]{1,0:T(8,128)(2,1)S(1)}, bf16[512,1024]{1,0:T(8,128)(2,1)}, u32[]{:S(2)}) copy-start(bf16[512,1024]{1,0:T(8,128)(2,1)} %param.12) | copy-start | bytes 3145732
  0.0 21.0 %collective-permute-start = (bf16[512,1024]{1,0:T(8,128)(2,1)}, bf16[512,1024]{1,0:T(8,128)(2,1)S(1)}, u32[]{:S(2)}, u32[]{:S(2)}) collective-permute-start(bf16[512,1024]{1,0:T(8,128)(2,1)} %refs_0_), channel_id=1, source_target_pairs={{4,8},{8,4},{0,0},{12,12},{5,9},{9,5},{1,1},{13,13},{6,10},{10,6},... | collective-permute-start | bytes 3145736 | tf_op jit(solution)/shard_map/ppermute | solution.py:285
  2.0 35.7 %collective-permute-start.3 = (bf16[512,1024]{1,0:T(8,128)(2,1)}, bf16[512,1024]{1,0:T(8,128)(2,1)S(1)}, u32[]{:S(2)}, u32[]{:S(2)}) collective-permute-start(bf16[512,1024]{1,0:T(8,128)(2,1)} %refs_0_), channel_id=1, source_target_pairs={{0,4},{4,0},{8,12},{12,8},{1,5},{5,1},{9,13},{13,9},{2,6},{6,2},{1... | collective-permute-start | bytes 3145736 | tf_op jit(solution)/shard_map/ppermute | solution.py:285
  8.1 27.2 %collective-permute-start.4 = (f32[64,512]{1,0:T(8,128)S(1)}, f32[64,512]{1,0:T(8,128)S(1)}, u32[]{:S(2)}, u32[]{:S(2)}) collective-permute-start(f32[64,512]{1,0:T(8,128)S(1)} %fusion.8), channel_id=1, source_target_pairs={{0,4},{4,0},{8,12},{12,8},{1,5},{5,1},{9,13},{13,9},{2,6},{6,2},{1... | collective-permute-start | bytes 393224 | tf_op jit(solution)/shard_map/ppermute | solution.py:285
  8.1 49.6 %collective-permute-start.2 = (bf16[512,1024]{1,0:T(8,128)(2,1)}, bf16[512,1024]{1,0:T(8,128)(2,1)S(1)}, u32[]{:S(2)}, u32[]{:S(2)}) collective-permute-start(bf16[512,1024]{1,0:T(8,128)(2,1)} %refs_0_), channel_id=1, source_target_pairs={{0,12},{12,0},{1,13},{13,1},{2,14},{14,2},{3,15},{15,3},{16,28},{2... | collective-permute-start | bytes 3145736 | tf_op jit(solution)/shard_map/ppermute | solution.py:285
  15.0 2.0 %copy-start.2 = (bf16[512,3584]{1,0:T(8,128)(2,1)S(1)}, bf16[512,3584]{1,0:T(8,128)(2,1)}, u32[]{:S(2)}) copy-start(bf16[512,3584]{1,0:T(8,128)(2,1)} %gate_ref) | copy-start | bytes 11010052
  17.1 20.6 %copy-start.6 = (bf16[64,4096]{1,0:T(8,128)(2,1)S(1)}, bf16[64,4096]{1,0:T(8,128)(2,1)}, u32[]{:S(2)}) copy-start(bf16[64,4096]{1,0:T(8,128)(2,1)} %param.18) | copy-start | bytes 1572868
  17.1 22.1 %copy-start.4 = (bf16[512,1024]{1,0:T(8,128)(2,1)S(1)}, bf16[512,1024]{1,0:T(8,128)(2,1)}, u32[]{:S(2)}) copy-start(bf16[512,1024]{1,0:T(8,128)(2,1)} %refs_0_) | copy-start | bytes 3145732
  21.1 46.3 %collective-permute-start.6 = (bf16[256,1024]{1,0:T(8,128)(2,1)S(1)}, bf16[256,1024]{1,0:T(8,128)(2,1)S(1)}, u32[]{:S(2)}, u32[]{:S(2)}) collective-permute-start(bf16[256,1024]{1,0:T(8,128)(2,1)S(1)} %get-tuple-element.31), channel_id=1, source_target_pairs={{0,8},{8,12},{12,4},{4,0},{1,9},{9,13},{13,5},{5,1},{2,10},{10,14}... | collective-permute-start | bytes 1572872 | tf_op jit(solution)/shard_map/ppermute | solution.py:285
  31.3 50.9 %collective-permute-start.1 = (bf16[256,1024]{1,0:T(8,128)(2,1)S(1)}, bf16[256,1024]{1,0:T(8,128)(2,1)S(1)}, u32[]{:S(2)}, u32[]{:S(2)}) collective-permute-start(bf16[256,1024]{1,0:T(8,128)(2,1)S(1)} %get-tuple-element.32), channel_id=1, source_target_pairs={{0,8},{8,12},{12,4},{4,0},{1,9},{9,13},{13,5},{5,1},{2,10},{10,14}... | collective-permute-start | bytes 1572872 | tf_op jit(solution)/shard_map/ppermute | solution.py:285
  35.3 15.7 %copy-start.7 = (s32[256]{0:T(256)S(1)}, s32[256]{0:T(256)}, u32[]{:S(2)}) copy-start(s32[256]{0:T(256)} %param.19) | copy-start | bytes 3076
  35.3 46.3 %collective-permute-start.7 = (f32[64,512]{1,0:T(8,128)S(1)}, f32[64,512]{1,0:T(8,128)S(1)}, u32[]{:S(2)}, u32[]{:S(2)}) collective-permute-start(f32[64,512]{1,0:T(8,128)S(1)} %add.37.refs_0_), channel_id=1, source_target_pairs={{0,12},{12,0},{4,8},{8,4},{1,13},{13,1},{5,9},{9,5},{2,14},{14,2},... | collective-permute-start | bytes 393224 | tf_op jit(solution)/shard_map/ppermute | solution.py:285
  37.7 13.3 %collective-permute-start.5 = (bf16[64,4096]{1,0:T(8,128)(2,1)S(1)}, bf16[64,4096]{1,0:T(8,128)(2,1)S(1)}, u32[]{:S(2)}, u32[]{:S(2)}) collective-permute-start(bf16[64,4096]{1,0:T(8,128)(2,1)S(1)} %copy-done.6), channel_id=1, source_target_pairs={{0,2},{2,0},{1,3},{3,1},{4,6},{6,4},{5,7},{7,5},{8,10},{10,8},{9,1... | collective-permute-start | bytes 1572872 | tf_op jit(solution)/shard_map/ppermute | solution.py:262
  67.5 7.9 %copy-start.3 = (bf16[3584,64]{0,1:T(8,128)(2,1)S(1)}, bf16[3584,64]{0,1:T(8,128)(2,1)}, u32[]{:S(2)}) copy-start(bf16[3584,64]{0,1:T(8,128)(2,1)} %param.16) | copy-start | bytes 1376260
  75.3 6.2 %copy-start.5 = (s32[1,512]{1,0:T(1,128)S(1)}, s32[1,512]{1,0:T(1,128)}, u32[]{:S(2)}) copy-start(s32[1,512]{1,0:T(1,128)} %seg_ref.1) | copy-start | bytes 6148
  82.2 17.0 %copy-start.1 = (bf16[512,1024]{1,0:T(8,128)(2,1)S(1)}, bf16[512,1024]{1,0:T(8,128)(2,1)}, u32[]{:S(2)}) copy-start(bf16[512,1024]{1,0:T(8,128)(2,1)} %param.12) | copy-start | bytes 3145732
  88.1 1.2 %collective-permute-start.8 = (f32[4,256]{1,0:T(4,128)S(1)}, f32[4,256]{1,0:T(4,128)S(1)}, u32[]{:S(2)}, u32[]{:S(2)}) collective-permute-start(f32[4,256]{1,0:T(4,128)S(1)} %shard_map.114), channel_id=1, source_target_pairs={{0,1},{1,0},{2,3},{3,2},{4,5},{5,4},{6,7},{7,6},{8,9},{9,8},{10,11... | collective-permute-start | bytes 12296 | tf_op jit(solution)/shard_map/ppermute | solution.py:22
  89.3 4.8 %collective-permute-start.9 = (f32[4,256]{1,0:T(4,128)S(1)}, f32[4,256]{1,0:T(4,128)S(1)}, u32[]{:S(2)}, u32[]{:S(2)}) collective-permute-start(f32[4,256]{1,0:T(4,128)S(1)} %add.44), channel_id=1, source_target_pairs={{0,4},{4,0},{8,12},{12,8},{1,5},{5,1},{9,13},{13,9},{2,6},{6,2},{1... | collective-permute-start | bytes 12296 | tf_op jit(solution)/shard_map/ppermute | solution.py:22
  94.1 4.5 %collective-permute-start.10 = (f32[4,256]{1,0:T(4,128)S(1)}, f32[4,256]{1,0:T(4,128)S(1)}, u32[]{:S(2)}, u32[]{:S(2)}) collective-permute-start(f32[4,256]{1,0:T(4,128)S(1)} %add.45), channel_id=1, source_target_pairs={{0,8},{4,12},{8,0},{12,4},{1,9},{5,13},{9,1},{13,5},{2,10},{6,14},... | collective-permute-start | bytes 12296 | tf_op jit(solution)/shard_map/ppermute | solution.py:22

commit v3 on v2

--- a/solution.py
+++ b/solution.py
@@ -78,7 +78,7 @@
         turn[...] = part[...].T
     mark_ref[...] = jnp.zeros_like(mark_ref)
 
-    @pl.loop(0, chunks)
+    @pl.loop(0, chunks, unroll=True)
     def _(chunk):
         rows = rows_of(total_ref, chunk)
         total = base_ref[rows, :] if has_base else 0.0
@@ -156,7 +156,7 @@
     turned[...] = part_ref[...].T
     out_ref[...] = jnp.zeros_like(out_ref)
 
-    @pl.loop(0, chunks_of(held_ref))
+    @pl.loop(0, chunks_of(held_ref), unroll=True)
     def _(chunk):
         rows = rows_of(held_ref, chunk)
         hidden = total_ref[rows, columns] + jnp.dot(
@@ -182,7 +182,7 @@
         cost_estimate=pl.CostEstimate(
             flops=2 * tokens * width * held.shape[0], bytes_accessed=2 * tokens * width, transcendentals=0
         ),
-    )(part, held_in_vmem(held), held_in_vmem(total), held_in_vmem(factor), proj)
+    )(*map(held_in_vmem, (part, held, total, factor, proj)))
 
 
 def last_kernel(
@@ -235,12 +235,12 @@
         cost_estimate=pl.CostEstimate(
             flops=2 * tokens * width * hidden, bytes_accessed=2 * tokens * width, transcendentals=0
         ),
-    )(part, *map(held_in_vmem, (held, total, factor)), proj, *map(held_in_vmem, (first, inside, bank)))
+    )(*map(held_in_vmem, (part, held, total, factor, proj, first, inside, bank)))
 
 
 def spread_kernel(seg_ref, *refs):
     inside_ref = refs[-1]
-    rows = sum(ref[...] for ref in refs[:-1])
+    rows = sum(ref[...].astype(jnp.float32) for ref in refs[:-1])
     for n in range(EX_DEV):
         columns = slice(n * rows.shape[0], (n + 1) * rows.shape[0])
         high, low = two_terms(jnp.where(seg_ref[...] == n, rows, 0.0).T)
@@ -283,6 +283,7 @@
     proj = proj_out.T
 
     send = lambda value, pairs: lax.ppermute(value, "tensor", pairs)
+    short = lambda value: value.astype(jnp.bfloat16)
     pick_of = lambda *t: jnp.asarray(t, jnp.int32)[me][None]
     project = lambda rows: lax.dot_general(
         proj_in, rows, (((0,), (1,)), ((), ())), preferred_element_type=jnp.float32
@@ -292,7 +293,7 @@
     in_part = project(layer_in)
     if tensor == 4:
         pairs, crossed, onward = [(0, 1), (1, 0), (2, 3), (3, 2)], [(0, 3), (3, 0)], [(0, 2), (2, 3), (3, 1), (1, 0)]
-        in_near = send(in_part, pairs)
+        in_near = send(short(in_part), pairs)
         middle = send(out_grad, [(1, 2), (2, 1), (0, 0), (3, 3)])
         near = send(out_grad, pairs)
         here = after(out_grad, in_part)
@@ -300,8 +301,9 @@
         factor = factors(after(gate_pre, in_part))
         middle = after(middle, factor)
         halves = [middle[:half], middle[half:]]
-        in_sum = in_part + after((in_near, in_part), *halves)[0]
-        in_rest = send(in_sum, crossed + [(1, 2), (2, 1)])
+        in_sum = in_part + after(in_near, *halves).astype(jnp.float32)
+        in_rest = send(short(in_sum), crossed + [(1, 2), (2, 1)])
+        halves[1] = after(halves[1], in_sum)
         far = [send(rows, onward) for rows in halves]
         near, query_bank = after((near, query_bank), in_sum)
         parts = bank_parts(query_bank, sizes["dp"])

time: 99.5 us -> 94 us (0.945)
  Pallas kernels: 33.5 us -> 30.3 us
  waiting for transfers between devices: 25.5 us -> 23.9 us
    pallas_call x1, Pallas kernels: 4.89 us -> 3.23 us  [first_terms(): pl.pallas_call(first_kernel, in_specs=[IN_VMEM] * 5, out_specs=IN_VMEM, s...]
    ppermute x7, waiting for transfers between devices: 20.8 us -> 19.1 us  [body(): send = lambda value, pairs: lax.ppermute(value, 'tensor', pairs)]
    pallas_call x1, Pallas kernels: 5.9 us -> 4.66 us  [last_scores(): pl.pallas_call(functools.partial(last_kernel, scale), in_specs=[IN_VMEM]...]
  transfers between devices with their start and end apart: 11 -> 11, of which waited for: 7 -> 6; matrix products, arithmetic and copies ran while one was open for 6% -> 7% of each run, Pallas kernels for 28% -> 27%
where the time goes in v3:
time: 94 us; the launch traced here: 93.8 us
  starting transfers between devices  30.3 us (32%)
  Pallas kernels  30.3 us (32%)
  waiting for transfers between devices  23.9 us (25%)
  local copies, waits for them, and re-layouts  4.71 us (5%)
  other arithmetic  2.27 us (2%)
  matrix products  2.11 us (2%)
    ppermute x7, starting transfers between devices, body(): send = lambda value, pairs: lax.ppermute(value, 'tensor', pairs)  23.4 us
    pallas_call x2, Pallas kernels, hidden_sum(): pl.pallas_call(functools.partial(hidden_kernel, blocks, bool(bases)), in_...  19.3 us
    ppermute x7, waiting for transfers between devices, body(): send = lambda value, pairs: lax.ppermute(value, 'tensor', pairs)  19.1 us
    ppermute x3, starting transfers between devices, sum_over(): lax.ppermute(value, axis, [(i, i ^ step) for i in range(size)])  5.36 us
    ppermute x3, waiting for transfers between devices, sum_over(): lax.ppermute(value, axis, [(i, i ^ step) for i in range(size)])  4.8 us
    pallas_call x1, Pallas kernels, last_scores(): pl.pallas_call(functools.partial(last_kernel, scale), in_specs=[IN_VMEM]...  4.66 us
    pallas_call x1, Pallas kernels, first_terms(): pl.pallas_call(first_kernel, in_specs=[IN_VMEM] * 5, out_specs=IN_VMEM, s...  3.23 us
    dynamic_slice x2, local copies, waits for them, and re-layouts, body(): pick_of = lambda *t: jnp.asarray(t, jnp.int32)[me][None]  2.57 us
  transfers between devices with their start and end apart: 11, of which 6 were waited for; matrix products, arithmetic and copies ran while one was open for 7% of the time, Pallas kernels for 27%

profile of v3, /device:TPU:0, one launch (start us, length us, event | category | flops | bytes accessed | tf_op | source)
XLA Modules:
  0.0 93.8 jit_solution(10496036990307653229)
XLA Ops:
  0.0 0.0 copy-start
  0.0 2.0 %collective-permute-start = (bf16[512,1024]{1,0:T(8,128)(2,1)}, bf16[512,1024]{1,0:T(8,128)(2,1)S(1)}, u32[]{:S(2)}, u32[]{:S(2)}) collective-permute-start(bf16[512,1024]{1,0:T(8,128)(2,1)} %refs_0_), channel_id=1, source_target_pairs={{4,8},{8,4},{0,0},{12,12},{5,9},{9,5},{1,1},{13,13},{6,10},{10,6},... | collective-permute-start | bytes 3145736 | tf_op jit(solution)/shard_map/ppermute | solution.py:285
  2.0 4.7 %collective-permute-start.4 = (bf16[512,1024]{1,0:T(8,128)(2,1)}, bf16[512,1024]{1,0:T(8,128)(2,1)S(1)}, u32[]{:S(2)}, u32[]{:S(2)}) collective-permute-start(bf16[512,1024]{1,0:T(8,128)(2,1)} %refs_0_), channel_id=1, source_target_pairs={{0,4},{4,0},{8,12},{12,8},{1,5},{5,1},{9,13},{13,9},{2,6},{6,2},{1... | collective-permute-start | bytes 3145736 | tf_op jit(solution)/shard_map/ppermute | solution.py:285
  6.7 0.0 copy-done
  6.7 1.3 %fusion.9 = (bf16[64,512]{1,0:T(8,128)(2,1)S(1)}, f32[64,512]{1,0:T(8,128)S(1)}) fusion(bf16[1024,64]{0,1:T(8,128)(2,1)} %param.15, bf16[512,1024]{1,0:T(8,128)(2,1)S(1)} %copy-done), kind=kOutput, calls=%fused_computation.17 | convolution fusion | flops 67141632 | bytes 1376256 | tf_op jit(solution)/shard_map/dot_general | solution.py:288
  8.1 0.1 collective-permute-start.1
  8.1 4.2 %collective-permute-start.3 = (bf16[512,1024]{1,0:T(8,128)(2,1)}, bf16[512,1024]{1,0:T(8,128)(2,1)S(1)}, u32[]{:S(2)}, u32[]{:S(2)}) collective-permute-start(bf16[512,1024]{1,0:T(8,128)(2,1)} %refs_0_), channel_id=1, source_target_pairs={{0,12},{12,0},{1,13},{13,1},{2,14},{14,2},{3,15},{15,3},{16,28},{2... | collective-permute-start | bytes 3145736 | tf_op jit(solution)/shard_map/ppermute | solution.py:285
  12.4 1.3 %dynamic_slice.7 = s32[1]{0:T(128)} dynamic-slice(s32[4]{0:T(128)} %constant.43.clone, s32[]{:T(128)S(6)} %select_n.23), dynamic_slice_sizes={1} | dynamic-slice | bytes 12 | tf_op jit(solution)/shard_map/dynamic_slice | solution.py:287
  13.7 1.3 %dynamic_slice.6 = s32[1]{0:T(128)} dynamic-slice(s32[4]{0:T(128)} %constant.42.clone, s32[]{:T(128)S(6)} %select_n.23), dynamic_slice_sizes={1} | dynamic-slice | bytes 12 | tf_op jit(solution)/shard_map/dynamic_slice | solution.py:287
  15.0 2.0 %copy-done.2 = bf16[512,3584]{1,0:T(8,128)(2,1)S(1)} copy-done((bf16[512,3584]{1,0:T(8,128)(2,1)S(1)}, bf16[512,3584]{1,0:T(8,128)(2,1)}, u32[]{:S(2)}) %copy-start.2) | copy-done | bytes 3670040
  17.1 2.5 %shard_map.109.factor_ref = f32[3584,512]{1,0:T(8,128)S(1)} custom-call(bf16[512,3584]{1,0:T(8,128)(2,1)S(1)} %copy-done.2), custom_call_target="tpu_custom_call" | custom-call | flops 14680064 | bytes 11010048 | tf_op jit(solution)/shard_map/pallas_call | solution.py:142
  19.6 0.1 pad_add_fusion.2.places_ref
  19.6 1.4 %pad_add_fusion.places_ref = s32[2]{0:T(128)S(1)} fusion(s32[1]{0:T(128)} %dynamic_slice.7, s32[1]{0:T(128)} %dynamic_slice.6), kind=kLoop, calls=%fused_computation.9 | loop fusion | flops 2 | bytes 16 | tf_op jit(solution)/shard_map/concatenate | solution.py:314
  21.0 0.1 pad_add_fusion.1
  21.1 0.0 collective-permute-done
  21.1 0.1 fusion.8
  21.2 10.1 %collective-permute-start.6 = (bf16[256,1024]{1,0:T(8,128)(2,1)S(1)}, bf16[256,1024]{1,0:T(8,128)(2,1)S(1)}, u32[]{:S(2)}, u32[]{:S(2)}) collective-permute-start(bf16[256,1024]{1,0:T(8,128)(2,1)S(1)} %get-tuple-element.35), channel_id=1, source_target_pairs={{0,8},{8,12},{12,4},{4,0},{1,9},{9,13},{13,5},{5,1},{2,10},{10,14}... | collective-permute-start | bytes 1572872 | tf_op jit(solution)/shard_map/ppermute | solution.py:285
  31.3 2.4 %collective-permute-done.1 = bf16[64,512]{1,0:T(8,128)(2,1)S(1)} collective-permute-done((bf16[64,512]{1,0:T(8,128)(2,1)S(1)}, bf16[64,512]{1,0:T(8,128)(2,1)S(1)}, u32[]{:S(2)}, u32[]{:S(2)}) %collective-permute-start.1) | collective-permute-done | bytes 65568 | tf_op jit(solution)/shard_map/ppermute | solution.py:285
  33.7 0.0 collective-permute-done.4.refs_1_
  33.7 0.0 copy-start.7
  33.7 2.1 %collective-permute-start.7 = (bf16[64,512]{1,0:T(8,128)(2,1)S(1)}, bf16[64,512]{1,0:T(8,128)(2,1)S(1)}, u32[]{:S(2)}, u32[]{:S(2)}) collective-permute-start(bf16[64,512]{1,0:T(8,128)(2,1)S(1)} %get-tuple-element.33), channel_id=1, source_target_pairs={{0,12},{12,0},{4,8},{8,4},{1,13},{13,1},{5,9},{9,5},{2,14},{14,2},... | collective-permute-start | bytes 196616 | tf_op jit(solution)/shard_map/ppermute | solution.py:285
  35.8 0.1 collective-permute-start.2
  36.0 0.0 copy-done.6
  36.0 1.5 %collective-permute-start.5 = (bf16[64,4096]{1,0:T(8,128)(2,1)S(1)}, bf16[64,4096]{1,0:T(8,128)(2,1)S(1)}, u32[]{:S(2)}, u32[]{:S(2)}) collective-permute-start(bf16[64,4096]{1,0:T(8,128)(2,1)S(1)} %copy-done.6), channel_id=1, source_target_pairs={{0,2},{2,0},{1,3},{3,1},{4,6},{6,4},{5,7},{7,5},{8,10},{10,8},{9,1... | collective-permute-start | bytes 1572872 | tf_op jit(solution)/shard_map/ppermute | solution.py:262
  37.5 0.0 copy-done.4
  37.5 11.5 %shard_map.110 = (f32[3584,512]{1,0:T(8,128)S(1)}, f32[8,128]{1,0:T(8,128)}, bf16[8,128]{1,0:T(8,128)(2,1)}) custom-call(s32[2]{0:T(128)S(1)} %pad_add_fusion.2.places_ref, bf16[3584,4096]{1,0:T(8,128)(2,1)} %weight_ref.3, bf16[512,1024]{1,0:T(8,128)(2,1)S(1)} %copy-done.4, bf16[512,1024]{1,0:T(8,128)(2,1)S(1)} %collective-permute-done.4.refs_1_), custom_call_target="tpu_custom_call" | custom-call | flops 7516192768 | bytes 16777216 | tf_op jit(solution)/shard_map/pallas_call | solution.py:106
  49.0 0.0 collective-permute-done.5
  49.0 0.0 copy-done.7
  49.0 0.8 convolution_convert_fusion.bank_ref
  49.8 6.5 %collective-permute-done.3 = bf16[512,1024]{1,0:T(8,128)(2,1)S(1)} collective-permute-done((bf16[512,1024]{1,0:T(8,128)(2,1)}, bf16[512,1024]{1,0:T(8,128)(2,1)S(1)}, u32[]{:S(2)}, u32[]{:S(2)}) %collective-permute-start.3) | collective-permute-done | bytes 1048608 | tf_op jit(solution)/shard_map/ppermute | solution.py:285
  56.3 0.1 broadcast_select_fusion.refs_0_
  56.4 10.2 %collective-permute-done.6.part_ref = bf16[256,1024]{1,0:T(8,128)(2,1)S(1)} collective-permute-done((bf16[256,1024]{1,0:T(8,128)(2,1)S(1)}, bf16[256,1024]{1,0:T(8,128)(2,1)S(1)}, u32[]{:S(2)}, u32[]{:S(2)}) %collective-permute-start.6) | collective-permute-done | bytes 524320 | tf_op jit(solution)/shard_map/ppermute | solution.py:285
  66.7 7.8 %shard_map.111 = (f32[3584,512]{1,0:T(8,128)S(1)}, f32[8,128]{1,0:T(8,128)}, bf16[3584,1024]{1,0:T(8,128)(2,1)S(1)}) custom-call(s32[2]{0:T(128)S(1)} %pad_add_fusion.places_ref, bf16[3584,4096]{1,0:T(8,128)(2,1)} %weight_ref.3, bf16[512,1024]{1,0:T(8,128)(2,1)S(1)} %broadcast_select_fusion.refs_0_, ...), custom_call_target="tpu_custom_call", output_to_operand_aliasing={{0}: (3, {})} | custom-call | flops 3758096384 | bytes 8388608 | tf_op jit(solution)/shard_map/pallas_call | solution.py:106
  74.4 0.0 copy-start.5
  74.4 3.2 %shard_map.112.first_ref = f32[64,256]{1,0:T(8,128)S(1)} custom-call(bf16[256,1024]{1,0:T(8,128)(2,1)S(1)} %collective-permute-done.6.part_ref, bf16[3584,1024]{1,0:T(8,128)(2,1)S(1)} %get-tuple-element.30.held_ref, f32[3584,512]{1,0:T(8,128)S(1)} %get-tuple-element.31.total_ref, f32[3584,512]{1,0:T(8,128)S(1)} %shard_map.109.factor_ref, ...), custom_call_target="tpu_custom_call" | custom-call | flops 1879048192 | bytes 524288 | tf_op jit(solution)/shard_map/pallas_call | solution.py:175
  77.7 0.0 collective-permute-done.7.refs_1_
  77.7 0.0 copy-done.5
  77.7 0.6 shard_map.113.inside_ref
  78.3 0.0 collective-permute-done.2.part_ref
  78.3 0.0 copy-start.1
  78.3 4.7 %shard_map.114 = f32[4,256]{1,0:T(4,128)S(1)} custom-call(bf16[256,1024]{1,0:T(8,128)(2,1)S(1)} %collective-permute-done.2.part_ref, bf16[3584,1024]{1,0:T(8,128)(2,1)S(1)} %get-tuple-element.30.held_ref, f32[3584,512]{1,0:T(8,128)S(1)} %get-tuple-element.31.total_ref, f32[3584,512]{1,0:T(8,128)S(1)} %shard_map.109.factor_ref, bf16[64,3584]{1,0:T(8,128)(2,1)S(1)} %bitcast.5, ...), custom_call_target="tpu_custom_call" | custom-call | flops 1879048192 | bytes 524288 | tf_op jit(solution)/shard_map/pallas_call | solution.py:222
  83.0 0.0 collective-permute-start.8
  83.0 1.2 %collective-permute-done.8 = f32[4,256]{1,0:T(4,128)S(1)} collective-permute-done((f32[4,256]{1,0:T(4,128)S(1)}, f32[4,256]{1,0:T(4,128)S(1)}, u32[]{:S(2)}, u32[]{:S(2)}) %collective-permute-start.8) | collective-permute-done | bytes 4128 | tf_op jit(solution)/shard_map/ppermute | solution.py:22
  84.2 2.9 %collective-permute-start.9 = (f32[4,256]{1,0:T(4,128)S(1)}, f32[4,256]{1,0:T(4,128)S(1)}, u32[]{:S(2)}, u32[]{:S(2)}) collective-permute-start(f32[4,256]{1,0:T(4,128)S(1)} %add.44), channel_id=1, source_target_pairs={{0,4},{4,0},{8,12},{12,8},{1,5},{5,1},{9,13},{13,9},{2,6},{6,2},{1... | collective-permute-start | bytes 12296 | tf_op jit(solution)/shard_map/ppermute | solution.py:22
  87.1 1.6 %collective-permute-done.9 = f32[4,256]{1,0:T(4,128)S(1)} collective-permute-done((f32[4,256]{1,0:T(4,128)S(1)}, f32[4,256]{1,0:T(4,128)S(1)}, u32[]{:S(2)}, u32[]{:S(2)}) %collective-permute-start.9) | collective-permute-done | bytes 4128 | tf_op jit(solution)/shard_map/ppermute | solution.py:22
  88.7 2.5 %collective-permute-start.10 = (f32[4,256]{1,0:T(4,128)S(1)}, f32[4,256]{1,0:T(4,128)S(1)}, u32[]{:S(2)}, u32[]{:S(2)}) collective-permute-start(f32[4,256]{1,0:T(4,128)S(1)} %add.45), channel_id=1, source_target_pairs={{0,8},{4,12},{8,0},{12,4},{1,9},{5,13},{9,1},{13,5},{2,10},{6,14},... | collective-permute-start | bytes 12296 | tf_op jit(solution)/shard_map/ppermute | solution.py:22
  91.1 2.0 %collective-permute-done.10 = f32[4,256]{1,0:T(4,128)S(1)} collective-permute-done((f32[4,256]{1,0:T(4,128)S(1)}, f32[4,256]{1,0:T(4,128)S(1)}, u32[]{:S(2)}, u32[]{:S(2)}) %collective-permute-start.10) | collective-permute-done | bytes 4128 | tf_op jit(solution)/shard_map/ppermute | solution.py:22
  93.2 0.6 add.46
  (10 shorter events, 0.0 us)
Async XLA Ops:
  0.0 6.7 %copy-start = (bf16[512,1024]{1,0:T(8,128)(2,1)S(1)}, bf16[512,1024]{1,0:T(8,128)(2,1)}, u32[]{:S(2)}) copy-start(bf16[512,1024]{1,0:T(8,128)(2,1)} %param.12) | copy-start | bytes 3145732
  0.0 21.1 %collective-permute-start = (bf16[512,1024]{1,0:T(8,128)(2,1)}, bf16[512,1024]{1,0:T(8,128)(2,1)S(1)}, u32[]{:S(2)}, u32[]{:S(2)}) collective-permute-start(bf16[512,1024]{1,0:T(8,128)(2,1)} %refs_0_), channel_id=1, source_target_pairs={{4,8},{8,4},{0,0},{12,12},{5,9},{9,5},{1,1},{13,13},{6,10},{10,6},... | collective-permute-start | bytes 3145736 | tf_op jit(solution)/shard_map/ppermute | solution.py:285
  2.0 31.7 %collective-permute-start.4 = (bf16[512,1024]{1,0:T(8,128)(2,1)}, bf16[512,1024]{1,0:T(8,128)(2,1)S(1)}, u32[]{:S(2)}, u32[]{:S(2)}) collective-permute-start(bf16[512,1024]{1,0:T(8,128)(2,1)} %refs_0_), channel_id=1, source_target_pairs={{0,4},{4,0},{8,12},{12,8},{1,5},{5,1},{9,13},{13,9},{2,6},{6,2},{1... | collective-permute-start | bytes 3145736 | tf_op jit(solution)/shard_map/ppermute | solution.py:285
  8.1 25.6 %collective-permute-start.1 = (bf16[64,512]{1,0:T(8,128)(2,1)S(1)}, bf16[64,512]{1,0:T(8,128)(2,1)S(1)}, u32[]{:S(2)}, u32[]{:S(2)}) collective-permute-start(bf16[64,512]{1,0:T(8,128)(2,1)S(1)} %get-tuple-element.37), channel_id=1, source_target_pairs={{0,4},{4,0},{8,12},{12,8},{1,5},{5,1},{9,13},{13,9},{2,6},{6,2},{1... | collective-permute-start | bytes 196616 | tf_op jit(solution)/shard_map/ppermute | solution.py:285
  8.1 48.2 %collective-permute-start.3 = (bf16[512,1024]{1,0:T(8,128)(2,1)}, bf16[512,1024]{1,0:T(8,128)(2,1)S(1)}, u32[]{:S(2)}, u32[]{:S(2)}) collective-permute-start(bf16[512,1024]{1,0:T(8,128)(2,1)} %refs_0_), channel_id=1, source_target_pairs={{0,12},{12,0},{1,13},{13,1},{2,14},{14,2},{3,15},{15,3},{16,28},{2... | collective-permute-start | bytes 3145736 | tf_op jit(solution)/shard_map/ppermute | solution.py:285
  15.0 2.0 %copy-start.2 = (bf16[512,3584]{1,0:T(8,128)(2,1)S(1)}, bf16[512,3584]{1,0:T(8,128)(2,1)}, u32[]{:S(2)}) copy-start(bf16[512,3584]{1,0:T(8,128)(2,1)} %gate_ref) | copy-start | bytes 11010052
  17.1 18.9 %copy-start.6 = (bf16[64,4096]{1,0:T(8,128)(2,1)S(1)}, bf16[64,4096]{1,0:T(8,128)(2,1)}, u32[]{:S(2)}) copy-start(bf16[64,4096]{1,0:T(8,128)(2,1)} %param.18) | copy-start | bytes 1572868
  17.1 20.4 %copy-start.4 = (bf16[512,1024]{1,0:T(8,128)(2,1)S(1)}, bf16[512,1024]{1,0:T(8,128)(2,1)}, u32[]{:S(2)}) copy-start(bf16[512,1024]{1,0:T(8,128)(2,1)} %refs_0_) | copy-start | bytes 3145732
  21.2 45.5 %collective-permute-start.6 = (bf16[256,1024]{1,0:T(8,128)(2,1)S(1)}, bf16[256,1024]{1,0:T(8,128)(2,1)S(1)}, u32[]{:S(2)}, u32[]{:S(2)}) collective-permute-start(bf16[256,1024]{1,0:T(8,128)(2,1)S(1)} %get-tuple-element.35), channel_id=1, source_target_pairs={{0,8},{8,12},{12,4},{4,0},{1,9},{9,13},{13,5},{5,1},{2,10},{10,14}... | collective-permute-start | bytes 1572872 | tf_op jit(solution)/shard_map/ppermute | solution.py:285
  33.7 15.3 %copy-start.7 = (s32[256]{0:T(256)S(1)}, s32[256]{0:T(256)}, u32[]{:S(2)}) copy-start(s32[256]{0:T(256)} %param.19) | copy-start | bytes 3076
  33.7 43.9 %collective-permute-start.7 = (bf16[64,512]{1,0:T(8,128)(2,1)S(1)}, bf16[64,512]{1,0:T(8,128)(2,1)S(1)}, u32[]{:S(2)}, u32[]{:S(2)}) collective-permute-start(bf16[64,512]{1,0:T(8,128)(2,1)S(1)} %get-tuple-element.33), channel_id=1, source_target_pairs={{0,12},{12,0},{4,8},{8,4},{1,13},{13,1},{5,9},{9,5},{2,14},{14,2},... | collective-permute-start | bytes 196616 | tf_op jit(solution)/shard_map/ppermute | solution.py:285
  35.8 42.5 %collective-permute-start.2 = (bf16[256,1024]{1,0:T(8,128)(2,1)S(1)}, bf16[256,1024]{1,0:T(8,128)(2,1)S(1)}, u32[]{:S(2)}, u32[]{:S(2)}) collective-permute-start(bf16[256,1024]{1,0:T(8,128)(2,1)S(1)} %get-tuple-element.22), channel_id=1, source_target_pairs={{0,8},{8,12},{12,4},{4,0},{1,9},{9,13},{13,5},{5,1},{2,10},{10,14}... | collective-permute-start | bytes 1572872 | tf_op jit(solution)/shard_map/ppermute | solution.py:285
  36.0 13.0 %collective-permute-start.5 = (bf16[64,4096]{1,0:T(8,128)(2,1)S(1)}, bf16[64,4096]{1,0:T(8,128)(2,1)S(1)}, u32[]{:S(2)}, u32[]{:S(2)}) collective-permute-start(bf16[64,4096]{1,0:T(8,128)(2,1)S(1)} %copy-done.6), channel_id=1, source_target_pairs={{0,2},{2,0},{1,3},{3,1},{4,6},{6,4},{5,7},{7,5},{8,10},{10,8},{9,1... | collective-permute-start | bytes 1572872 | tf_op jit(solution)/shard_map/ppermute | solution.py:262
  66.7 7.8 %copy-start.3 = (bf16[3584,64]{0,1:T(8,128)(2,1)S(1)}, bf16[3584,64]{0,1:T(8,128)(2,1)}, u32[]{:S(2)}) copy-start(bf16[3584,64]{0,1:T(8,128)(2,1)} %param.16) | copy-start | bytes 1376260
  74.4 3.3 %copy-start.5 = (s32[1,512]{1,0:T(1,128)S(1)}, s32[1,512]{1,0:T(1,128)}, u32[]{:S(2)}) copy-start(s32[1,512]{1,0:T(1,128)} %seg_ref.1) | copy-start | bytes 6148
  78.3 15.4 %copy-start.1 = (bf16[512,1024]{1,0:T(8,128)(2,1)S(1)}, bf16[512,1024]{1,0:T(8,128)(2,1)}, u32[]{:S(2)}) copy-start(bf16[512,1024]{1,0:T(8,128)(2,1)} %param.12) | copy-start | bytes 3145732
  83.0 1.2 %collective-permute-start.8 = (f32[4,256]{1,0:T(4,128)S(1)}, f32[4,256]{1,0:T(4,128)S(1)}, u32[]{:S(2)}, u32[]{:S(2)}) collective-permute-start(f32[4,256]{1,0:T(4,128)S(1)} %shard_map.114), channel_id=1, source_target_pairs={{0,1},{1,0},{2,3},{3,2},{4,5},{5,4},{6,7},{7,6},{8,9},{9,8},{10,11... | collective-permute-start | bytes 12296 | tf_op jit(solution)/shard_map/ppermute | solution.py:22
  84.2 4.5 %collective-permute-start.9 = (f32[4,256]{1,0:T(4,128)S(1)}, f32[4,256]{1,0:T(4,128)S(1)}, u32[]{:S(2)}, u32[]{:S(2)}) collective-permute-start(f32[4,256]{1,0:T(4,128)S(1)} %add.44), channel_id=1, source_target_pairs={{0,4},{4,0},{8,12},{12,8},{1,5},{5,1},{9,13},{13,9},{2,6},{6,2},{1... | collective-permute-start | bytes 12296 | tf_op jit(solution)/shard_map/ppermute | solution.py:22
  88.7 4.5 %collective-permute-start.10 = (f32[4,256]{1,0:T(4,128)S(1)}, f32[4,256]{1,0:T(4,128)S(1)}, u32[]{:S(2)}, u32[]{:S(2)}) collective-permute-start(f32[4,256]{1,0:T(4,128)S(1)} %add.45), channel_id=1, source_target_pairs={{0,8},{4,12},{8,0},{12,4},{1,9},{5,13},{9,1},{13,5},{2,10},{6,14},... | collective-permute-start | bytes 12296 | tf_op jit(solution)/shard_map/ppermute | solution.py:22

commit v4 on v3

--- a/solution.py
+++ b/solution.py
@@ -8,6 +8,7 @@
 from jax.sharding import PartitionSpec as P
 
 EX_DEV = 4
+COST = 2
 TILE = 512
 EXACT = lax.Precision.HIGHEST
 
@@ -35,7 +36,7 @@
 
 IN_VMEM = pl.BlockSpec(memory_space=pltpu.VMEM)
 IN_SMEM = pl.BlockSpec(memory_space=pltpu.SMEM)
-ANYWHERE = pl.BlockSpec(memory_space=pl.ANY)
+IN_HBM = pl.BlockSpec(memory_space=pltpu.HBM)
 
 
 def column_copy(weight_ref, place, held_ref, sem_ref, chunk):
@@ -58,7 +59,7 @@
     return pl.ds(pl.multiple_of(chunk * tile, tile), tile)
 
 
-def hidden_kernel(blocks, has_base, places_ref, weight_ref, *refs):
+def hidden_kernel(blocks, has_base, keeps, places_ref, weight_ref, *refs):
     parts, refs = refs[:blocks], refs[blocks:]
     base_ref, refs = (refs[0], refs[1:]) if has_base else (None, refs)
     total_ref, mark_ref, kept_ref, refs = refs[0], refs[1], refs[2], refs[3:]
@@ -70,7 +71,7 @@
         for k in range(blocks):
             column_copy(weight_ref, places_ref[k], held[k], sems[k], chunk).start()
 
-    @pl.loop(0, chunks if has_base else 0)
+    @pl.loop(0, chunks if keeps else 0)
     def _(chunk):
         column_copy(weight_ref, places_ref[blocks], kept_ref, kept_sem, chunk).start()
 
@@ -87,7 +88,7 @@
             total += jnp.dot(held[k][rows, :], turned[k][...], preferred_element_type=jnp.float32)
         total_ref[rows, :] = total
 
-    @pl.loop(0, chunks if has_base else 0)
+    @pl.loop(0, chunks if keeps else 0)
     def _(chunk):
         column_copy(weight_ref, places_ref[blocks], kept_ref, kept_sem, chunk).wait()
 
@@ -96,16 +97,16 @@
     return pltpu.with_memory_space_constraint(value, pltpu.VMEM)
 
 
-def hidden_sum(parts, places, weight, base=None):
+def hidden_sum(parts, places, weight, base=None, keeps=False):
     tokens, width = parts[0].shape
     hidden = weight.shape[0]
     blocks = len(parts)
     bases = [] if base is None else [held_in_vmem(base)]
-    kept = (hidden, width) if bases else (8, 128)
+    kept = (hidden, width) if keeps else (8, 128)
     chunks = pltpu.SemaphoreType.DMA((hidden // tile_of(hidden),))
     return pl.pallas_call(
-        functools.partial(hidden_kernel, blocks, bool(bases)),
-        in_specs=[IN_SMEM, ANYWHERE] + [IN_VMEM] * (blocks + len(bases)),
+        functools.partial(hidden_kernel, blocks, bool(bases), keeps),
+        in_specs=[IN_SMEM, IN_HBM] + [IN_VMEM] * (blocks + len(bases)),
         out_specs=[IN_VMEM] * 3,
         scratch_shapes=[pltpu.VMEM((hidden, width), weight.dtype)] * blocks
         + [pltpu.VMEM((width, tokens), parts[0].dtype)] * blocks
@@ -118,11 +119,11 @@
         input_output_aliases={2 + blocks: 0} if bases else {},
         compiler_params=pltpu.CompilerParams(vmem_limit_bytes=(6 + 9 * blocks) << 20),
         cost_estimate=pl.CostEstimate(
-            flops=2 * blocks * tokens * width * hidden,
-            bytes_accessed=2 * blocks * width * (tokens + hidden),
+            flops=int(COST * blocks * tokens * width * hidden),
+            bytes_accessed=int(COST * blocks * width * (tokens + hidden)),
             transcendentals=0,
         ),
-    )(places, weight, *parts, *bases)
+    )(places, pltpu.with_memory_space_constraint(weight, pltpu.HBM), *parts, *bases)
 
 
 def silu(gate):
@@ -166,8 +167,8 @@
         out_ref[...] += jnp.dot(proj_ref[:, rows], up, preferred_element_type=jnp.float32)
 
 
-def first_kernel(part_ref, held_ref, total_ref, factor_ref, proj_ref, out_ref, turned):
-    term_loop(part_ref, held_ref, total_ref, factor_ref, proj_ref, out_ref, turned, 0)
+def first_kernel(*refs):
+    term_loop(*refs, 0)
 
 
 def first_terms(part, held, total, factor, proj):
@@ -292,43 +293,43 @@
     half = out_grad.shape[0] // 2
     in_part = project(layer_in)
     if tensor == 4:
-        pairs, crossed, onward = [(0, 1), (1, 0), (2, 3), (3, 2)], [(0, 3), (3, 0)], [(0, 2), (2, 3), (3, 1), (1, 0)]
+        pairs, onward = [(0, 1), (1, 0), (2, 3), (3, 2)], [(0, 2), (2, 3), (3, 1), (1, 0)]
         in_near = send(short(in_part), pairs)
-        middle = send(out_grad, [(1, 2), (2, 1), (0, 0), (3, 3)])
+        inner = send(out_grad, [(1, 2), (2, 1), (0, 0), (3, 3)])
         near = send(out_grad, pairs)
-        here = after(out_grad, in_part)
-        cross = send(here, crossed)
         factor = factors(after(gate_pre, in_part))
-        middle = after(middle, factor)
-        halves = [middle[:half], middle[half:]]
+        total, mark, _ = hidden_sum([after(out_grad, factor)], me[None], down_weight)
+        inner = after(inner, mark)
+        halves = [inner[:half], inner[half:]]
+        far = [send(rows, onward) for rows in halves]
         in_sum = in_part + after(in_near, *halves).astype(jnp.float32)
-        in_rest = send(short(in_sum), crossed + [(1, 2), (2, 1)])
-        halves[1] = after(halves[1], in_sum)
-        far = [send(rows, onward) for rows in halves]
+        in_rest = send(short(in_sum), [(0, 3), (3, 0), (1, 2), (2, 1)])
         near, query_bank = after((near, query_bank), in_sum)
         parts = bank_parts(query_bank, sizes["dp"])
-        total, mark, _ = hidden_sum([here, near], jnp.concatenate([me[None], me[None] ^ 1]), down_weight)
-        bank = picked(after(parts, mark), query_ids)
-        cross = after(cross, bank)
-        rest = jnp.where((me == 0) | (me == 3), cross, middle)
-        places = jnp.concatenate([pick_of(3, 2, 1, 0), pick_of(2, 3, 0, 1)])
-        total, mark, held = hidden_sum([rest], places, down_weight, total)
+        total, mark, _ = hidden_sum([near], me[None] ^ 1, down_weight, total)
         far[0] = after(far[0], mark)
+        outer = [send(far[0], pairs)]
+        far[1] = after(far[1], far[0])
+        outer.append(send(far[1], pairs))
+        bank = picked(after(parts, far[1]), query_ids)
+        places = jnp.concatenate([pick_of(2, 3, 0, 1), pick_of(3, 2, 1, 0)])
+        total, mark, held = hidden_sum([jnp.concatenate(far)], places, down_weight, total, True)
+        outer[0] = after(outer[0], mark)
     else:
         in_sum, in_rest = sum_over(in_part, "tensor", tensor), jnp.zeros_like(in_part)
         factor = factors(gate_pre)
         gathered = lax.all_gather(out_grad, "tensor", axis=1, tiled=True)
         step = gathered.shape[1] // 4
         blocks = [gathered[:, k * step : (k + 1) * step] for k in range(4)]
-        far = [blocks[3][:half], blocks[3][half:]]
+        outer = [blocks[3][:half], blocks[3][half:]]
         places = jnp.arange(4, dtype=jnp.int32)
         total, _, _ = hidden_sum(blocks[:2], places[:2], down_weight)
-        total, _, held = hidden_sum(blocks[2:3], places[2:], down_weight, total)
+        total, _, held = hidden_sum(blocks[2:3], places[2:], down_weight, total, True)
         bank = picked(bank_parts(query_bank, sizes["dp"]), query_ids)
 
-    first = first_terms(far[0], held, total, factor, proj)
+    first = first_terms(outer[0], held, total, factor, proj)
     inside = spread(segment_ids, in_sum, after(in_rest, first))
-    scores = last_scores(far[1], held, total, factor, proj, first, inside, bank, scale)
+    scores = last_scores(outer[1], held, total, factor, proj, first, inside, bank, scale)
     scores = sum_over(scores, "seq", sizes["seq"])
     return sum_over(scores, "tensor", tensor)
 

time: 94 us -> 92.3 us (0.982)
  starting transfers between devices: 30.3 us -> 24.8 us
  local copies, waits for them, and re-layouts: 4.71 us -> 7.54 us
  Pallas kernels: 30.3 us -> 32 us
    ppermute x7 -> x8, starting transfers between devices: 23.4 us -> 19.8 us  [body(): send = lambda value, pairs: lax.ppermute(value, 'tensor', pairs)]
    unnamed x16 -> x22, local copies, waits for them, and re-layouts: 2.07 us -> 4.99 us
    ppermute x3, starting transfers between devices: 5.36 us -> 3.45 us  [sum_over(): lax.ppermute(value, axis, [(i, i ^ step) for i in range(size)])]
    pallas_call x2 -> x3, Pallas kernels: 19.3 us -> 21 us  [hidden_sum(): pl.pallas_call(functools.partial(hidden_kernel, blocks, bool(bases), keep...]
    ppermute x7 -> x8, waiting for transfers between devices: 19.1 us -> 17.6 us  [body(): send = lambda value, pairs: lax.ppermute(value, 'tensor', pairs)]
    ppermute x3, waiting for transfers between devices: 4.8 us -> 5.84 us  [sum_over(): lax.ppermute(value, axis, [(i, i ^ step) for i in range(size)])]
  transfers between devices with their start and end apart: 11 -> 12, of which waited for: 6 -> 7; matrix products, arithmetic and copies ran while one was open for 7% -> 7% of each run, Pallas kernels for 27% -> 30%
where the time goes in v4:
time: 92.3 us; the launch traced here: 92.1 us
  Pallas kernels  32 us (35%)
  starting transfers between devices  24.8 us (27%)
  waiting for transfers between devices  23.4 us (25%)
  local copies, waits for them, and re-layouts  7.54 us (8%)
  matrix products  2.12 us (2%)
  other arithmetic  2.02 us (2%)
    pallas_call x3, Pallas kernels, hidden_sum(): pl.pallas_call(functools.partial(hidden_kernel, blocks, bool(bases), keep...  21 us
    ppermute x8, starting transfers between devices, body(): send = lambda value, pairs: lax.ppermute(value, 'tensor', pairs)  19.8 us
    ppermute x8, waiting for transfers between devices, body(): send = lambda value, pairs: lax.ppermute(value, 'tensor', pairs)  17.6 us
    ppermute x3, waiting for transfers between devices, sum_over(): lax.ppermute(value, axis, [(i, i ^ step) for i in range(size)])  5.84 us
    unnamed x22, local copies, waits for them, and re-layouts  4.99 us
    pallas_call x1, Pallas kernels, last_scores(): pl.pallas_call(functools.partial(last_kernel, scale), in_specs=[IN_VMEM]...  4.66 us
    ppermute x3, starting transfers between devices, sum_over(): lax.ppermute(value, axis, [(i, i ^ step) for i in range(size)])  3.45 us
    pallas_call x1, Pallas kernels, first_terms(): pl.pallas_call(first_kernel, in_specs=[IN_VMEM] * 5, out_specs=IN_VMEM, s...  3.23 us
  transfers between devices with their start and end apart: 12, of which 7 were waited for; matrix products, arithmetic and copies ran while one was open for 7% of the time, Pallas kernels for 30%

profile of v4, /device:TPU:0, one launch (start us, length us, event | category | flops | bytes accessed | tf_op | source)
XLA Modules:
  0.0 92.1 jit_solution(2333859772423509070)
XLA Ops:
  0.0 2.0 %collective-permute-start = (bf16[512,1024]{1,0:T(8,128)(2,1)}, bf16[512,1024]{1,0:T(8,128)(2,1)S(1)}, u32[]{:S(2)}, u32[]{:S(2)}) collective-permute-start(bf16[512,1024]{1,0:T(8,128)(2,1)} %refs_0_), channel_id=1, source_target_pairs={{4,8},{8,4},{0,0},{12,12},{5,9},{9,5},{1,1},{13,13},{6,10},{10,6},... | collective-permute-start | bytes 3145736 | tf_op jit(solution)/shard_map/ppermute | solution.py:286
  2.0 4.7 %collective-permute-start.4 = (bf16[512,1024]{1,0:T(8,128)(2,1)}, bf16[512,1024]{1,0:T(8,128)(2,1)S(1)}, u32[]{:S(2)}, u32[]{:S(2)}) collective-permute-start(bf16[512,1024]{1,0:T(8,128)(2,1)} %refs_0_), channel_id=1, source_target_pairs={{0,4},{4,0},{8,12},{12,8},{1,5},{5,1},{9,13},{13,9},{2,6},{6,2},{1... | collective-permute-start | bytes 3145736 | tf_op jit(solution)/shard_map/ppermute | solution.py:286
  6.7 1.3 %fusion.9 = (bf16[64,512]{1,0:T(8,128)(2,1)S(1)}, f32[64,512]{1,0:T(8,128)S(1)}) fusion(bf16[1024,64]{0,1:T(8,128)(2,1)} %param.15, bf16[512,1024]{1,0:T(8,128)(2,1)S(1)} %copy-done), kind=kOutput, calls=%fused_computation.16 | convolution fusion | flops 67141632 | bytes 1376256 | tf_op jit(solution)/shard_map/dot_general | solution.py:289
  8.1 0.1 collective-permute-start.5
  8.2 1.2 %dynamic_slice.6 = s32[1]{0:T(128)} dynamic-slice(s32[4]{0:T(128)} %constant.40.clone, s32[]{:T(128)S(6)} %select_n.15), dynamic_slice_sizes={1} | dynamic-slice | bytes 12 | tf_op jit(solution)/shard_map/dynamic_slice | solution.py:288
  9.4 1.3 %dynamic_slice.7 = s32[1]{0:T(128)} dynamic-slice(s32[4]{0:T(128)} %constant.41.clone, s32[]{:T(128)S(6)} %select_n.15), dynamic_slice_sizes={1} | dynamic-slice | bytes 12 | tf_op jit(solution)/shard_map/dynamic_slice | solution.py:288
  10.6 2.0 %copy-done.3 = bf16[512,3584]{1,0:T(8,128)(2,1)S(1)} copy-done((bf16[512,3584]{1,0:T(8,128)(2,1)S(1)}, bf16[512,3584]{1,0:T(8,128)(2,1)}, u32[]{:S(2)}) %copy-start.3) | copy-done | bytes 3670040
  12.7 2.5 %shard_map.109.refs_3_.factor_ref = f32[3584,512]{1,0:T(8,128)S(1)} custom-call(bf16[512,3584]{1,0:T(8,128)(2,1)S(1)} %copy-done.3), custom_call_target="tpu_custom_call" | custom-call | flops 14680064 | bytes 11010048 | tf_op jit(solution)/shard_map/pallas_call | solution.py:143
  15.2 2.9 %copy-done.2 = f32[3584,512]{1,0:T(8,128)} copy-done((f32[3584,512]{1,0:T(8,128)}, f32[3584,512]{1,0:T(8,128)S(1)}, u32[]{:S(2)}) %copy-start.2) | copy-done | bytes 7340056
  18.1 6.4 %shard_map.110 = (f32[3584,512]{1,0:T(8,128)S(1)}, f32[8,128]{1,0:T(8,128)}, bf16[8,128]{1,0:T(8,128)(2,1)}) custom-call(s32[1]{0:T(128)} %bitcast.places_ref, bf16[3584,4096]{1,0:T(8,128)(2,1)} %weight_ref.5, bf16[512,1024]{1,0:T(8,128)(2,1)S(1)} %copy-done.5), custom_call_target="tpu_custom_call" | custom-call | flops 3758096384 | bytes 8388608 | tf_op jit(solution)/shard_map/pallas_call | solution.py:107
  24.5 0.0 collective-permute-done
  24.5 0.1 fusion.8
  24.6 6.7 %collective-permute-start.2 = (bf16[256,1024]{1,0:T(8,128)(2,1)S(1)}, bf16[256,1024]{1,0:T(8,128)(2,1)S(1)}, u32[]{:S(2)}, u32[]{:S(2)}) collective-permute-start(bf16[256,1024]{1,0:T(8,128)(2,1)S(1)} %get-tuple-element.33), channel_id=1, source_target_pairs={{0,8},{8,12},{12,4},{4,0},{1,9},{9,13},{13,5},{5,1},{2,10},{10,14}... | collective-permute-start | bytes 1572872 | tf_op jit(solution)/shard_map/ppermute | solution.py:286
  31.3 0.1 collective-permute-start.1
  31.4 0.9 collective-permute-done.5
  32.3 0.0 collective-permute-done.4.refs_0_
  32.3 0.0 copy-done.7
  32.3 1.6 %collective-permute-start.8 = (bf16[64,4096]{1,0:T(8,128)(2,1)S(1)}, bf16[64,4096]{1,0:T(8,128)(2,1)S(1)}, u32[]{:S(2)}, u32[]{:S(2)}) collective-permute-start(bf16[64,4096]{1,0:T(8,128)(2,1)S(1)} %copy-done.7), channel_id=1, source_target_pairs={{0,2},{2,0},{1,3},{3,1},{4,6},{6,4},{5,7},{7,5},{8,10},{10,8},{9,1... | collective-permute-start | bytes 1572872 | tf_op jit(solution)/shard_map/ppermute | solution.py:263
  33.8 1.3 %pad_add_fusion.places_ref = s32[2]{0:T(128)S(1)} fusion(s32[1]{0:T(128)} %dynamic_slice.7, s32[1]{0:T(128)} %dynamic_slice.6), kind=kLoop, calls=%fused_computation.9 | loop fusion | flops 2 | bytes 16 | tf_op jit(solution)/shard_map/concatenate | solution.py:315
  35.1 0.1 pad_add_fusion.1
  35.2 2.3 %collective-permute-start.7 = (bf16[64,512]{1,0:T(8,128)(2,1)S(1)}, bf16[64,512]{1,0:T(8,128)(2,1)S(1)}, u32[]{:S(2)}, u32[]{:S(2)}) collective-permute-start(bf16[64,512]{1,0:T(8,128)(2,1)S(1)} %get-tuple-element.31), channel_id=1, source_target_pairs={{0,12},{12,0},{4,8},{8,4},{1,13},{13,1},{5,9},{9,5},{2,14},{14,2},... | collective-permute-start | bytes 196616 | tf_op jit(solution)/shard_map/ppermute | solution.py:286
  37.4 6.6 %shard_map.111 = (f32[3584,512]{1,0:T(8,128)S(1)}, f32[8,128]{1,0:T(8,128)}, bf16[8,128]{1,0:T(8,128)(2,1)}) custom-call(s32[1]{0:T(128)S(6)} %xor.3.places_ref, bf16[3584,4096]{1,0:T(8,128)(2,1)} %weight_ref.5, bf16[512,1024]{1,0:T(8,128)(2,1)S(1)} %collective-permute-done.4.refs_0_, ...), custom_call_target="tpu_custom_call", output_to_operand_aliasing={{0}: (3, {})} | custom-call | flops 3758096384 | bytes 8388608 | tf_op jit(solution)/shard_map/pallas_call | solution.py:107
  44.0 0.0 collective-permute-done.2
  44.0 2.1 %collective-permute-start.6 = (bf16[256,1024]{1,0:T(8,128)(2,1)S(1)}, bf16[256,1024]{1,0:T(8,128)(2,1)S(1)}, u32[]{:S(2)}, u32[]{:S(2)}) collective-permute-start(bf16[256,1024]{1,0:T(8,128)(2,1)S(1)} %collective-permute-done.2), channel_id=1, source_target_pairs={{0,4},{4,0},{8,12},{12,8},{1,5},{5,1},{9,13},{13,9},{2,6},{6,2},{1... | collective-permute-start | bytes 1572872 | tf_op jit(solution)/shard_map/ppermute | solution.py:286
  46.1 9.3 %collective-permute-done.1 = bf16[256,1024]{1,0:T(8,128)(2,1)S(1)} collective-permute-done((bf16[256,1024]{1,0:T(8,128)(2,1)S(1)}, bf16[256,1024]{1,0:T(8,128)(2,1)S(1)}, u32[]{:S(2)}, u32[]{:S(2)}) %collective-permute-start.1) | collective-permute-done | bytes 524320 | tf_op jit(solution)/shard_map/ppermute | solution.py:286
  55.4 1.9 %collective-permute-start.3 = (bf16[256,1024]{1,0:T(8,128)(2,1)S(1)}, bf16[256,1024]{1,0:T(8,128)(2,1)S(1)}, u32[]{:S(2)}, u32[]{:S(2)}) collective-permute-start(bf16[256,1024]{1,0:T(8,128)(2,1)S(1)} %collective-permute-done.1), channel_id=1, source_target_pairs={{0,4},{4,0},{8,12},{12,8},{1,5},{5,1},{9,13},{13,9},{2,6},{6,2},{1... | collective-permute-start | bytes 1572872 | tf_op jit(solution)/shard_map/ppermute | solution.py:286
  57.3 0.0 collective-permute-done.8
  57.3 0.8 convolution_convert_fusion.bank_ref
  58.1 0.1 pad_maximum_fusion.refs_0_
  58.2 0.0 slice-start
  58.2 0.0 slice-start.1
  58.2 0.0 copy-start.4
  58.2 8.0 %shard_map.112 = (f32[3584,512]{1,0:T(8,128)S(1)}, f32[8,128]{1,0:T(8,128)}, bf16[3584,1024]{1,0:T(8,128)(2,1)S(1)}) custom-call(s32[2]{0:T(128)S(1)} %pad_add_fusion.places_ref, bf16[3584,4096]{1,0:T(8,128)(2,1)} %weight_ref.5, bf16[512,1024]{1,0:T(8,128)(2,1)S(1)} %pad_maximum_fusion.refs_0_, ...), custom_call_target="tpu_custom_call", output_to_operand_aliasing={{0}: (3, {})} | custom-call | flops 3758096384 | bytes 8388608 | tf_op jit(solution)/shard_map/pallas_call | solution.py:107
  66.3 1.3 %collective-permute-done.6.refs_0_ = bf16[256,1024]{1,0:T(8,128)(2,1)S(1)} collective-permute-done((bf16[256,1024]{1,0:T(8,128)(2,1)S(1)}, bf16[256,1024]{1,0:T(8,128)(2,1)S(1)}, u32[]{:S(2)}, u32[]{:S(2)}) %collective-permute-start.6) | collective-permute-done | bytes 524320 | tf_op jit(solution)/shard_map/ppermute | solution.py:286
  67.6 0.0 slice-done.1
  67.6 0.0 copy-start.6
  67.6 3.2 %shard_map.113.first_ref = f32[64,256]{1,0:T(8,128)S(1)} custom-call(bf16[256,1024]{1,0:T(8,128)(2,1)S(1)} %collective-permute-done.6.refs_0_, bf16[3584,1024]{1,0:T(8,128)(2,1)S(1)} %get-tuple-element.25.refs_1_.held_ref, f32[3584,512]{1,0:T(8,128)S(1)} %get-tuple-element.26.refs_2_.total_ref, f32[3584,512]{1,0:T(8,128)S(1)} %bitcast.5, ...), custom_call_target="tpu_custom_call" | custom-call | flops 1879048192 | bytes 524288 | tf_op jit(solution)/shard_map/pallas_call | solution.py:176
  70.9 0.0 collective-permute-done.7.refs_1_
  70.9 0.6 shard_map.114.inside_ref
  71.5 6.0 %collective-permute-done.3.part_ref = bf16[256,1024]{1,0:T(8,128)(2,1)S(1)} collective-permute-done((bf16[256,1024]{1,0:T(8,128)(2,1)S(1)}, bf16[256,1024]{1,0:T(8,128)(2,1)S(1)}, u32[]{:S(2)}, u32[]{:S(2)}) %collective-permute-start.3) | collective-permute-done | bytes 524320 | tf_op jit(solution)/shard_map/ppermute | solution.py:286
  77.6 4.7 %shard_map.115 = f32[4,256]{1,0:T(4,128)S(1)} custom-call(bf16[256,1024]{1,0:T(8,128)(2,1)S(1)} %collective-permute-done.3.part_ref, bf16[3584,1024]{1,0:T(8,128)(2,1)S(1)} %get-tuple-element.25.refs_1_.held_ref, f32[3584,512]{1,0:T(8,128)S(1)} %get-tuple-element.26.refs_2_.total_ref, f32[3584,512]{1,0:T(8,128)S(1)} %bitcast.5, ...), custom_call_target="tpu_custom_call" | custom-call | flops 1879048192 | bytes 524288 | tf_op jit(solution)/shard_map/pallas_call | solution.py:223
  82.2 0.0 collective-permute-start.9
  82.2 1.2 %collective-permute-done.9 = f32[4,256]{1,0:T(4,128)S(1)} collective-permute-done((f32[4,256]{1,0:T(4,128)S(1)}, f32[4,256]{1,0:T(4,128)S(1)}, u32[]{:S(2)}, u32[]{:S(2)}) %collective-permute-start.9) | collective-permute-done | bytes 4128 | tf_op jit(solution)/shard_map/ppermute | solution.py:23
  83.4 1.8 %collective-permute-start.10 = (f32[4,256]{1,0:T(4,128)S(1)}, f32[4,256]{1,0:T(4,128)S(1)}, u32[]{:S(2)}, u32[]{:S(2)}) collective-permute-start(f32[4,256]{1,0:T(4,128)S(1)} %add.44), channel_id=1, source_target_pairs={{0,4},{4,0},{8,12},{12,8},{1,5},{5,1},{9,13},{13,9},{2,6},{6,2},{1... | collective-permute-start | bytes 12296 | tf_op jit(solution)/shard_map/ppermute | solution.py:23
  85.2 1.8 %collective-permute-done.10 = f32[4,256]{1,0:T(4,128)S(1)} collective-permute-done((f32[4,256]{1,0:T(4,128)S(1)}, f32[4,256]{1,0:T(4,128)S(1)}, u32[]{:S(2)}, u32[]{:S(2)}) %collective-permute-start.10) | collective-permute-done | bytes 4128 | tf_op jit(solution)/shard_map/ppermute | solution.py:23
  87.0 1.7 %collective-permute-start.11 = (f32[4,256]{1,0:T(4,128)S(1)}, f32[4,256]{1,0:T(4,128)S(1)}, u32[]{:S(2)}, u32[]{:S(2)}) collective-permute-start(f32[4,256]{1,0:T(4,128)S(1)} %add.45), channel_id=1, source_target_pairs={{0,8},{4,12},{8,0},{12,4},{1,9},{5,13},{9,1},{13,5},{2,10},{6,14},... | collective-permute-start | bytes 12296 | tf_op jit(solution)/shard_map/ppermute | solution.py:23
  88.7 2.8 %collective-permute-done.11 = f32[4,256]{1,0:T(4,128)S(1)} collective-permute-done((f32[4,256]{1,0:T(4,128)S(1)}, f32[4,256]{1,0:T(4,128)S(1)}, u32[]{:S(2)}, u32[]{:S(2)}) %collective-permute-start.11) | collective-permute-done | bytes 4128 | tf_op jit(solution)/shard_map/ppermute | solution.py:23
  91.5 0.6 add.46
  (19 shorter events, 0.1 us)
Async XLA Ops:
  0.0 6.7 %copy-start = (bf16[512,1024]{1,0:T(8,128)(2,1)S(1)}, bf16[512,1024]{1,0:T(8,128)(2,1)}, u32[]{:S(2)}) copy-start(bf16[512,1024]{1,0:T(8,128)(2,1)} %param.12) | copy-start | bytes 3145732
  0.0 24.5 %collective-permute-start = (bf16[512,1024]{1,0:T(8,128)(2,1)}, bf16[512,1024]{1,0:T(8,128)(2,1)S(1)}, u32[]{:S(2)}, u32[]{:S(2)}) collective-permute-start(bf16[512,1024]{1,0:T(8,128)(2,1)} %refs_0_), channel_id=1, source_target_pairs={{4,8},{8,4},{0,0},{12,12},{5,9},{9,5},{1,1},{13,13},{6,10},{10,6},... | collective-permute-start | bytes 3145736 | tf_op jit(solution)/shard_map/ppermute | solution.py:286
  2.0 30.3 %collective-permute-start.4 = (bf16[512,1024]{1,0:T(8,128)(2,1)}, bf16[512,1024]{1,0:T(8,128)(2,1)S(1)}, u32[]{:S(2)}, u32[]{:S(2)}) collective-permute-start(bf16[512,1024]{1,0:T(8,128)(2,1)} %refs_0_), channel_id=1, source_target_pairs={{0,4},{4,0},{8,12},{12,8},{1,5},{5,1},{9,13},{13,9},{2,6},{6,2},{1... | collective-permute-start | bytes 3145736 | tf_op jit(solution)/shard_map/ppermute | solution.py:286
  8.1 24.2 %collective-permute-start.5 = (bf16[64,512]{1,0:T(8,128)(2,1)S(1)}, bf16[64,512]{1,0:T(8,128)(2,1)S(1)}, u32[]{:S(2)}, u32[]{:S(2)}) collective-permute-start(bf16[64,512]{1,0:T(8,128)(2,1)S(1)} %get-tuple-element.35), channel_id=1, source_target_pairs={{0,4},{4,0},{8,12},{12,8},{1,5},{5,1},{9,13},{13,9},{2,6},{6,2},{1... | collective-permute-start | bytes 196616 | tf_op jit(solution)/shard_map/ppermute | solution.py:286
  10.6 2.0 %copy-start.3 = (bf16[512,3584]{1,0:T(8,128)(2,1)S(1)}, bf16[512,3584]{1,0:T(8,128)(2,1)}, u32[]{:S(2)}) copy-start(bf16[512,3584]{1,0:T(8,128)(2,1)} %gate_ref) | copy-start | bytes 11010052
  12.7 5.4 %copy-start.5 = (bf16[512,1024]{1,0:T(8,128)(2,1)S(1)}, bf16[512,1024]{1,0:T(8,128)(2,1)}, u32[]{:S(2)}) copy-start(bf16[512,1024]{1,0:T(8,128)(2,1)} %refs_0_) | copy-start | bytes 3145732
  15.2 2.9 %copy-start.2 = (f32[3584,512]{1,0:T(8,128)}, f32[3584,512]{1,0:T(8,128)S(1)}, u32[]{:S(2)}) copy-start(f32[3584,512]{1,0:T(8,128)S(1)} %shard_map.109.refs_3_.factor_ref) | copy-start | bytes 22020100
  18.1 14.2 %copy-start.7 = (bf16[64,4096]{1,0:T(8,128)(2,1)S(1)}, bf16[64,4096]{1,0:T(8,128)(2,1)}, u32[]{:S(2)}) copy-start(bf16[64,4096]{1,0:T(8,128)(2,1)} %param.18) | copy-start | bytes 1572868
  24.6 19.5 %collective-permute-start.2 = (bf16[256,1024]{1,0:T(8,128)(2,1)S(1)}, bf16[256,1024]{1,0:T(8,128)(2,1)S(1)}, u32[]{:S(2)}, u32[]{:S(2)}) collective-permute-start(bf16[256,1024]{1,0:T(8,128)(2,1)S(1)} %get-tuple-element.33), channel_id=1, source_target_pairs={{0,8},{8,12},{12,4},{4,0},{1,9},{9,13},{13,5},{5,1},{2,10},{10,14}... | collective-permute-start | bytes 1572872 | tf_op jit(solution)/shard_map/ppermute | solution.py:286
  31.3 24.1 %collective-permute-start.1 = (bf16[256,1024]{1,0:T(8,128)(2,1)S(1)}, bf16[256,1024]{1,0:T(8,128)(2,1)S(1)}, u32[]{:S(2)}, u32[]{:S(2)}) collective-permute-start(bf16[256,1024]{1,0:T(8,128)(2,1)S(1)} %get-tuple-element.34), channel_id=1, source_target_pairs={{0,8},{8,12},{12,4},{4,0},{1,9},{9,13},{13,5},{5,1},{2,10},{10,14}... | collective-permute-start | bytes 1572872 | tf_op jit(solution)/shard_map/ppermute | solution.py:286
  32.3 25.0 %collective-permute-start.8 = (bf16[64,4096]{1,0:T(8,128)(2,1)S(1)}, bf16[64,4096]{1,0:T(8,128)(2,1)S(1)}, u32[]{:S(2)}, u32[]{:S(2)}) collective-permute-start(bf16[64,4096]{1,0:T(8,128)(2,1)S(1)} %copy-done.7), channel_id=1, source_target_pairs={{0,2},{2,0},{1,3},{3,1},{4,6},{6,4},{5,7},{7,5},{8,10},{10,8},{9,1... | collective-permute-start | bytes 1572872 | tf_op jit(solution)/shard_map/ppermute | solution.py:263
  35.2 35.7 %collective-permute-start.7 = (bf16[64,512]{1,0:T(8,128)(2,1)S(1)}, bf16[64,512]{1,0:T(8,128)(2,1)S(1)}, u32[]{:S(2)}, u32[]{:S(2)}) collective-permute-start(bf16[64,512]{1,0:T(8,128)(2,1)S(1)} %get-tuple-element.31), channel_id=1, source_target_pairs={{0,12},{12,0},{4,8},{8,4},{1,13},{13,1},{5,9},{9,5},{2,14},{14,2},... | collective-permute-start | bytes 196616 | tf_op jit(solution)/shard_map/ppermute | solution.py:286
  37.4 19.9 %copy-start.8 = (s32[256]{0:T(256)S(1)}, s32[256]{0:T(256)}, u32[]{:S(2)}) copy-start(s32[256]{0:T(256)} %param.19) | copy-start | bytes 3076
  44.0 23.5 %collective-permute-start.6 = (bf16[256,1024]{1,0:T(8,128)(2,1)S(1)}, bf16[256,1024]{1,0:T(8,128)(2,1)S(1)}, u32[]{:S(2)}, u32[]{:S(2)}) collective-permute-start(bf16[256,1024]{1,0:T(8,128)(2,1)S(1)} %collective-permute-done.2), channel_id=1, source_target_pairs={{0,4},{4,0},{8,12},{12,8},{1,5},{5,1},{9,13},{13,9},{2,6},{6,2},{1... | collective-permute-start | bytes 1572872 | tf_op jit(solution)/shard_map/ppermute | solution.py:286
  55.4 22.1 %collective-permute-start.3 = (bf16[256,1024]{1,0:T(8,128)(2,1)S(1)}, bf16[256,1024]{1,0:T(8,128)(2,1)S(1)}, u32[]{:S(2)}, u32[]{:S(2)}) collective-permute-start(bf16[256,1024]{1,0:T(8,128)(2,1)S(1)} %collective-permute-done.1), channel_id=1, source_target_pairs={{0,4},{4,0},{8,12},{12,8},{1,5},{5,1},{9,13},{13,9},{2,6},{6,2},{1... | collective-permute-start | bytes 1572872 | tf_op jit(solution)/shard_map/ppermute | solution.py:286
  58.2 9.4 %slice-start = ((s8[7340032]{0:T(1024)(128)(4,1)}), s8[4194304]{0:T(1024)(128)(4,1)S(1)}, s32[]{:S(2)}) async-start(s8[7340032]{0:T(1024)(128)(4,1)} %bitcast.4), calls=%async_computation | async-start | bytes 8388608
  58.2 9.4 %slice-start.1 = ((s8[7340032]{0:T(1024)(128)(4,1)}), s8[3145728]{0:T(1024)(128)(4,1)S(1)}, s32[]{:S(2)}) async-start(s8[7340032]{0:T(1024)(128)(4,1)} %bitcast.4), calls=%async_computation.1 | async-start | bytes 6291456
  58.2 9.4 %copy-start.4 = (bf16[3584,64]{0,1:T(8,128)(2,1)S(1)}, bf16[3584,64]{0,1:T(8,128)(2,1)}, u32[]{:S(2)}) copy-start(bf16[3584,64]{0,1:T(8,128)(2,1)} %param.16) | copy-start | bytes 1376260
  67.6 3.3 %copy-start.6 = (s32[1,512]{1,0:T(1,128)S(1)}, s32[1,512]{1,0:T(1,128)}, u32[]{:S(2)}) copy-start(s32[1,512]{1,0:T(1,128)} %seg_ref.1) | copy-start | bytes 6148
  77.5 14.6 %copy-start.1 = (bf16[512,1024]{1,0:T(8,128)(2,1)S(1)}, bf16[512,1024]{1,0:T(8,128)(2,1)}, u32[]{:S(2)}) copy-start(bf16[512,1024]{1,0:T(8,128)(2,1)} %param.12) | copy-start | bytes 3145732
  82.2 1.2 %collective-permute-start.9 = (f32[4,256]{1,0:T(4,128)S(1)}, f32[4,256]{1,0:T(4,128)S(1)}, u32[]{:S(2)}, u32[]{:S(2)}) collective-permute-start(f32[4,256]{1,0:T(4,128)S(1)} %shard_map.115), channel_id=1, source_target_pairs={{0,1},{1,0},{2,3},{3,2},{4,5},{5,4},{6,7},{7,6},{8,9},{9,8},{10,11... | collective-permute-start | bytes 12296 | tf_op jit(solution)/shard_map/ppermute | solution.py:23
  83.4 3.6 %collective-permute-start.10 = (f32[4,256]{1,0:T(4,128)S(1)}, f32[4,256]{1,0:T(4,128)S(1)}, u32[]{:S(2)}, u32[]{:S(2)}) collective-permute-start(f32[4,256]{1,0:T(4,128)S(1)} %add.44), channel_id=1, source_target_pairs={{0,4},{4,0},{8,12},{12,8},{1,5},{5,1},{9,13},{13,9},{2,6},{6,2},{1... | collective-permute-start | bytes 12296 | tf_op jit(solution)/shard_map/ppermute | solution.py:23
  87.0 4.5 %collective-permute-start.11 = (f32[4,256]{1,0:T(4,128)S(1)}, f32[4,256]{1,0:T(4,128)S(1)}, u32[]{:S(2)}, u32[]{:S(2)}) collective-permute-start(f32[4,256]{1,0:T(4,128)S(1)} %add.45), channel_id=1, source_target_pairs={{0,8},{4,12},{8,0},{12,4},{1,9},{5,13},{9,1},{13,5},{2,10},{6,14},... | collective-permute-start | bytes 12296 | tf_op jit(solution)/shard_map/ppermute | solution.py:23

commit v5 on v4

--- a/solution.py
+++ b/solution.py
@@ -212,8 +212,9 @@
         flat_ref[(n + 1) * half : (n + 2) * half] = jnp.where(left, pltpu.roll(even, width, 1), odd)
     flat = jnp.concatenate([flat_ref[pl.ds(p, EX_DEV, stride=half), :] for p in range(half)], axis=1)
     bank = bank_ref[...]
-    found = sum(jnp.dot(t, bank, preferred_element_type=jnp.float32) for t in two_terms(flat))
-    scores_ref[...] = scale * found
+    terms = jnp.concatenate([t.astype(jnp.float32) for t in two_terms(flat)]).astype(jnp.bfloat16)
+    found = jnp.dot(terms, bank, preferred_element_type=jnp.float32)
+    scores_ref[...] = scale * (found[:EX_DEV] + found[EX_DEV:])
 
 
 def last_scores(part, held, total, factor, proj, first, inside, bank, scale):

time: 92.3 us -> 91.6 us (level)
  no operation moved by 1% of the time
where the time goes in v5:
time: 91.6 us; the launch traced here: 91.4 us
  Pallas kernels  31.3 us (34%)
  starting transfers between devices  24.8 us (27%)
  waiting for transfers between devices  23.4 us (26%)
  local copies, waits for them, and re-layouts  7.54 us (8%)
  matrix products  2.12 us (2%)
  other arithmetic  2.02 us (2%)
    pallas_call x3, Pallas kernels, hidden_sum(): pl.pallas_call(functools.partial(hidden_kernel, blocks, bool(bases), keep...  21 us
    ppermute x8, starting transfers between devices, body(): send = lambda value, pairs: lax.ppermute(value, 'tensor', pairs)  19.8 us
    ppermute x8, waiting for transfers between devices, body(): send = lambda value, pairs: lax.ppermute(value, 'tensor', pairs)  17.6 us
    ppermute x3, waiting for transfers between devices, sum_over(): lax.ppermute(value, axis, [(i, i ^ step) for i in range(size)])  5.84 us
    unnamed x22, local copies, waits for them, and re-layouts  4.99 us
    pallas_call x1, Pallas kernels, last_scores(): pl.pallas_call(functools.partial(last_kernel, scale), in_specs=[IN_VMEM]...  3.92 us
    ppermute x3, starting transfers between devices, sum_over(): lax.ppermute(value, axis, [(i, i ^ step) for i in range(size)])  3.45 us
    pallas_call x1, Pallas kernels, first_terms(): pl.pallas_call(first_kernel, in_specs=[IN_VMEM] * 5, out_specs=IN_VMEM, s...  3.23 us
  transfers between devices with their start and end apart: 12, of which 7 were waited for; matrix products, arithmetic and copies ran while one was open for 7% of the time, Pallas kernels for 30%

profile of v5, /device:TPU:0, one launch (start us, length us, event | category | flops | bytes accessed | tf_op | source)
XLA Modules:
  0.0 91.4 jit_solution(3199073142816506096)
XLA Ops:
  0.0 2.0 %collective-permute-start = (bf16[512,1024]{1,0:T(8,128)(2,1)}, bf16[512,1024]{1,0:T(8,128)(2,1)S(1)}, u32[]{:S(2)}, u32[]{:S(2)}) collective-permute-start(bf16[512,1024]{1,0:T(8,128)(2,1)} %refs_0_), channel_id=1, source_target_pairs={{4,8},{8,4},{0,0},{12,12},{5,9},{9,5},{1,1},{13,13},{6,10},{10,6},... | collective-permute-start | bytes 3145736 | tf_op jit(solution)/shard_map/ppermute | solution.py:287
  2.0 4.7 %collective-permute-start.4 = (bf16[512,1024]{1,0:T(8,128)(2,1)}, bf16[512,1024]{1,0:T(8,128)(2,1)S(1)}, u32[]{:S(2)}, u32[]{:S(2)}) collective-permute-start(bf16[512,1024]{1,0:T(8,128)(2,1)} %refs_0_), channel_id=1, source_target_pairs={{0,4},{4,0},{8,12},{12,8},{1,5},{5,1},{9,13},{13,9},{2,6},{6,2},{1... | collective-permute-start | bytes 3145736 | tf_op jit(solution)/shard_map/ppermute | solution.py:287
  6.7 1.3 %fusion.9 = (bf16[64,512]{1,0:T(8,128)(2,1)S(1)}, f32[64,512]{1,0:T(8,128)S(1)}) fusion(bf16[1024,64]{0,1:T(8,128)(2,1)} %param.15, bf16[512,1024]{1,0:T(8,128)(2,1)S(1)} %copy-done), kind=kOutput, calls=%fused_computation.16 | convolution fusion | flops 67141632 | bytes 1376256 | tf_op jit(solution)/shard_map/dot_general | solution.py:290
  8.1 0.1 collective-permute-start.5
  8.2 1.2 %dynamic_slice.6 = s32[1]{0:T(128)} dynamic-slice(s32[4]{0:T(128)} %constant.40.clone, s32[]{:T(128)S(6)} %select_n.15), dynamic_slice_sizes={1} | dynamic-slice | bytes 12 | tf_op jit(solution)/shard_map/dynamic_slice | solution.py:289
  9.4 1.3 %dynamic_slice.7 = s32[1]{0:T(128)} dynamic-slice(s32[4]{0:T(128)} %constant.41.clone, s32[]{:T(128)S(6)} %select_n.15), dynamic_slice_sizes={1} | dynamic-slice | bytes 12 | tf_op jit(solution)/shard_map/dynamic_slice | solution.py:289
  10.6 2.0 %copy-done.3 = bf16[512,3584]{1,0:T(8,128)(2,1)S(1)} copy-done((bf16[512,3584]{1,0:T(8,128)(2,1)S(1)}, bf16[512,3584]{1,0:T(8,128)(2,1)}, u32[]{:S(2)}) %copy-start.3) | copy-done | bytes 3670040
  12.7 2.5 %shard_map.109.refs_3_.factor_ref = f32[3584,512]{1,0:T(8,128)S(1)} custom-call(bf16[512,3584]{1,0:T(8,128)(2,1)S(1)} %copy-done.3), custom_call_target="tpu_custom_call" | custom-call | flops 14680064 | bytes 11010048 | tf_op jit(solution)/shard_map/pallas_call | solution.py:143
  15.2 2.9 %copy-done.2 = f32[3584,512]{1,0:T(8,128)} copy-done((f32[3584,512]{1,0:T(8,128)}, f32[3584,512]{1,0:T(8,128)S(1)}, u32[]{:S(2)}) %copy-start.2) | copy-done | bytes 7340056
  18.1 6.4 %shard_map.110 = (f32[3584,512]{1,0:T(8,128)S(1)}, f32[8,128]{1,0:T(8,128)}, bf16[8,128]{1,0:T(8,128)(2,1)}) custom-call(s32[1]{0:T(128)} %bitcast.places_ref, bf16[3584,4096]{1,0:T(8,128)(2,1)} %weight_ref.5, bf16[512,1024]{1,0:T(8,128)(2,1)S(1)} %copy-done.5), custom_call_target="tpu_custom_call" | custom-call | flops 3758096384 | bytes 8388608 | tf_op jit(solution)/shard_map/pallas_call | solution.py:107
  24.5 0.0 collective-permute-done
  24.5 0.1 fusion.8
  24.6 6.7 %collective-permute-start.2 = (bf16[256,1024]{1,0:T(8,128)(2,1)S(1)}, bf16[256,1024]{1,0:T(8,128)(2,1)S(1)}, u32[]{:S(2)}, u32[]{:S(2)}) collective-permute-start(bf16[256,1024]{1,0:T(8,128)(2,1)S(1)} %get-tuple-element.33), channel_id=1, source_target_pairs={{0,8},{8,12},{12,4},{4,0},{1,9},{9,13},{13,5},{5,1},{2,10},{10,14}... | collective-permute-start | bytes 1572872 | tf_op jit(solution)/shard_map/ppermute | solution.py:287
  31.3 0.1 collective-permute-start.1
  31.4 0.9 collective-permute-done.5
  32.3 0.0 collective-permute-done.4.refs_0_
  32.3 1.6 %collective-permute-start.8 = (bf16[64,4096]{1,0:T(8,128)(2,1)S(1)}, bf16[64,4096]{1,0:T(8,128)(2,1)S(1)}, u32[]{:S(2)}, u32[]{:S(2)}) collective-permute-start(bf16[64,4096]{1,0:T(8,128)(2,1)S(1)} %copy-done.7), channel_id=1, source_target_pairs={{0,2},{2,0},{1,3},{3,1},{4,6},{6,4},{5,7},{7,5},{8,10},{10,8},{9,1... | collective-permute-start | bytes 1572872 | tf_op jit(solution)/shard_map/ppermute | solution.py:264
  33.8 1.3 %pad_add_fusion.places_ref = s32[2]{0:T(128)S(1)} fusion(s32[1]{0:T(128)} %dynamic_slice.7, s32[1]{0:T(128)} %dynamic_slice.6), kind=kLoop, calls=%fused_computation.9 | loop fusion | flops 2 | bytes 16 | tf_op jit(solution)/shard_map/concatenate | solution.py:316
  35.1 0.1 pad_add_fusion.1
  35.2 2.3 %collective-permute-start.7 = (bf16[64,512]{1,0:T(8,128)(2,1)S(1)}, bf16[64,512]{1,0:T(8,128)(2,1)S(1)}, u32[]{:S(2)}, u32[]{:S(2)}) collective-permute-start(bf16[64,512]{1,0:T(8,128)(2,1)S(1)} %get-tuple-element.31), channel_id=1, source_target_pairs={{0,12},{12,0},{4,8},{8,4},{1,13},{13,1},{5,9},{9,5},{2,14},{14,2},... | collective-permute-start | bytes 196616 | tf_op jit(solution)/shard_map/ppermute | solution.py:287
  37.4 6.6 %shard_map.111 = (f32[3584,512]{1,0:T(8,128)S(1)}, f32[8,128]{1,0:T(8,128)}, bf16[8,128]{1,0:T(8,128)(2,1)}) custom-call(s32[1]{0:T(128)S(6)} %xor.3.places_ref, bf16[3584,4096]{1,0:T(8,128)(2,1)} %weight_ref.5, bf16[512,1024]{1,0:T(8,128)(2,1)S(1)} %collective-permute-done.4.refs_0_, ...), custom_call_target="tpu_custom_call", output_to_operand_aliasing={{0}: (3, {})} | custom-call | flops 3758096384 | bytes 8388608 | tf_op jit(solution)/shard_map/pallas_call | solution.py:107
  44.0 0.0 collective-permute-done.2
  44.0 2.1 %collective-permute-start.6 = (bf16[256,1024]{1,0:T(8,128)(2,1)S(1)}, bf16[256,1024]{1,0:T(8,128)(2,1)S(1)}, u32[]{:S(2)}, u32[]{:S(2)}) collective-permute-start(bf16[256,1024]{1,0:T(8,128)(2,1)S(1)} %collective-permute-done.2), channel_id=1, source_target_pairs={{0,4},{4,0},{8,12},{12,8},{1,5},{5,1},{9,13},{13,9},{2,6},{6,2},{1... | collective-permute-start | bytes 1572872 | tf_op jit(solution)/shard_map/ppermute | solution.py:287
  46.1 9.3 %collective-permute-done.1 = bf16[256,1024]{1,0:T(8,128)(2,1)S(1)} collective-permute-done((bf16[256,1024]{1,0:T(8,128)(2,1)S(1)}, bf16[256,1024]{1,0:T(8,128)(2,1)S(1)}, u32[]{:S(2)}, u32[]{:S(2)}) %collective-permute-start.1) | collective-permute-done | bytes 524320 | tf_op jit(solution)/shard_map/ppermute | solution.py:287
  55.4 1.9 %collective-permute-start.3 = (bf16[256,1024]{1,0:T(8,128)(2,1)S(1)}, bf16[256,1024]{1,0:T(8,128)(2,1)S(1)}, u32[]{:S(2)}, u32[]{:S(2)}) collective-permute-start(bf16[256,1024]{1,0:T(8,128)(2,1)S(1)} %collective-permute-done.1), channel_id=1, source_target_pairs={{0,4},{4,0},{8,12},{12,8},{1,5},{5,1},{9,13},{13,9},{2,6},{6,2},{1... | collective-permute-start | bytes 1572872 | tf_op jit(solution)/shard_map/ppermute | solution.py:287
  57.3 0.0 collective-permute-done.8
  57.3 0.0 copy-done.8
  57.3 0.8 convolution_convert_fusion.bank_ref
  58.1 0.1 pad_maximum_fusion.refs_0_
  58.2 0.0 slice-start
  58.2 0.0 slice-start.1
  58.2 0.0 copy-start.4
  58.2 8.0 %shard_map.112 = (f32[3584,512]{1,0:T(8,128)S(1)}, f32[8,128]{1,0:T(8,128)}, bf16[3584,1024]{1,0:T(8,128)(2,1)S(1)}) custom-call(s32[2]{0:T(128)S(1)} %pad_add_fusion.places_ref, bf16[3584,4096]{1,0:T(8,128)(2,1)} %weight_ref.5, bf16[512,1024]{1,0:T(8,128)(2,1)S(1)} %pad_maximum_fusion.refs_0_, ...), custom_call_target="tpu_custom_call", output_to_operand_aliasing={{0}: (3, {})} | custom-call | flops 3758096384 | bytes 8388608 | tf_op jit(solution)/shard_map/pallas_call | solution.py:107
  66.3 1.3 %collective-permute-done.6.refs_0_ = bf16[256,1024]{1,0:T(8,128)(2,1)S(1)} collective-permute-done((bf16[256,1024]{1,0:T(8,128)(2,1)S(1)}, bf16[256,1024]{1,0:T(8,128)(2,1)S(1)}, u32[]{:S(2)}, u32[]{:S(2)}) %collective-permute-start.6) | collective-permute-done | bytes 524320 | tf_op jit(solution)/shard_map/ppermute | solution.py:287
  67.6 0.0 slice-done
  67.6 0.0 copy-start.6
  67.6 3.2 %shard_map.113.first_ref = f32[64,256]{1,0:T(8,128)S(1)} custom-call(bf16[256,1024]{1,0:T(8,128)(2,1)S(1)} %collective-permute-done.6.refs_0_, bf16[3584,1024]{1,0:T(8,128)(2,1)S(1)} %get-tuple-element.25.refs_1_.held_ref, f32[3584,512]{1,0:T(8,128)S(1)} %get-tuple-element.26.refs_2_.total_ref, f32[3584,512]{1,0:T(8,128)S(1)} %bitcast.5, ...), custom_call_target="tpu_custom_call" | custom-call | flops 1879048192 | bytes 524288 | tf_op jit(solution)/shard_map/pallas_call | solution.py:176
  70.9 0.0 collective-permute-done.7.refs_1_
  70.9 0.6 shard_map.114.inside_ref
  71.5 6.0 %collective-permute-done.3.part_ref = bf16[256,1024]{1,0:T(8,128)(2,1)S(1)} collective-permute-done((bf16[256,1024]{1,0:T(8,128)(2,1)S(1)}, bf16[256,1024]{1,0:T(8,128)(2,1)S(1)}, u32[]{:S(2)}, u32[]{:S(2)}) %collective-permute-start.3) | collective-permute-done | bytes 524320 | tf_op jit(solution)/shard_map/ppermute | solution.py:287
  77.6 3.9 %shard_map.115 = f32[4,256]{1,0:T(4,128)S(1)} custom-call(bf16[256,1024]{1,0:T(8,128)(2,1)S(1)} %collective-permute-done.3.part_ref, bf16[3584,1024]{1,0:T(8,128)(2,1)S(1)} %get-tuple-element.25.refs_1_.held_ref, f32[3584,512]{1,0:T(8,128)S(1)} %get-tuple-element.26.refs_2_.total_ref, f32[3584,512]{1,0:T(8,128)S(1)} %bitcast.5, ...), custom_call_target="tpu_custom_call" | custom-call | flops 1879048192 | bytes 524288 | tf_op jit(solution)/shard_map/pallas_call | solution.py:224
  81.5 0.0 collective-permute-start.9
  81.5 1.2 %collective-permute-done.9 = f32[4,256]{1,0:T(4,128)S(1)} collective-permute-done((f32[4,256]{1,0:T(4,128)S(1)}, f32[4,256]{1,0:T(4,128)S(1)}, u32[]{:S(2)}, u32[]{:S(2)}) %collective-permute-start.9) | collective-permute-done | bytes 4128 | tf_op jit(solution)/shard_map/ppermute | solution.py:23
  82.7 1.8 %collective-permute-start.10 = (f32[4,256]{1,0:T(4,128)S(1)}, f32[4,256]{1,0:T(4,128)S(1)}, u32[]{:S(2)}, u32[]{:S(2)}) collective-permute-start(f32[4,256]{1,0:T(4,128)S(1)} %add.44), channel_id=1, source_target_pairs={{0,4},{4,0},{8,12},{12,8},{1,5},{5,1},{9,13},{13,9},{2,6},{6,2},{1... | collective-permute-start | bytes 12296 | tf_op jit(solution)/shard_map/ppermute | solution.py:23
  84.4 1.8 %collective-permute-done.10 = f32[4,256]{1,0:T(4,128)S(1)} collective-permute-done((f32[4,256]{1,0:T(4,128)S(1)}, f32[4,256]{1,0:T(4,128)S(1)}, u32[]{:S(2)}, u32[]{:S(2)}) %collective-permute-start.10) | collective-permute-done | bytes 4128 | tf_op jit(solution)/shard_map/ppermute | solution.py:23
  86.3 1.7 %collective-permute-start.11 = (f32[4,256]{1,0:T(4,128)S(1)}, f32[4,256]{1,0:T(4,128)S(1)}, u32[]{:S(2)}, u32[]{:S(2)}) collective-permute-start(f32[4,256]{1,0:T(4,128)S(1)} %add.45), channel_id=1, source_target_pairs={{0,8},{4,12},{8,0},{12,4},{1,9},{5,13},{9,1},{13,5},{2,10},{6,14},... | collective-permute-start | bytes 12296 | tf_op jit(solution)/shard_map/ppermute | solution.py:23
  87.9 2.8 %collective-permute-done.11 = f32[4,256]{1,0:T(4,128)S(1)} collective-permute-done((f32[4,256]{1,0:T(4,128)S(1)}, f32[4,256]{1,0:T(4,128)S(1)}, u32[]{:S(2)}, u32[]{:S(2)}) %collective-permute-start.11) | collective-permute-done | bytes 4128 | tf_op jit(solution)/shard_map/ppermute | solution.py:23
  90.8 0.6 add.46
  (19 shorter events, 0.1 us)
Async XLA Ops:
  0.0 6.7 %copy-start = (bf16[512,1024]{1,0:T(8,128)(2,1)S(1)}, bf16[512,1024]{1,0:T(8,128)(2,1)}, u32[]{:S(2)}) copy-start(bf16[512,1024]{1,0:T(8,128)(2,1)} %param.12) | copy-start | bytes 3145732
  0.0 24.5 %collective-permute-start = (bf16[512,1024]{1,0:T(8,128)(2,1)}, bf16[512,1024]{1,0:T(8,128)(2,1)S(1)}, u32[]{:S(2)}, u32[]{:S(2)}) collective-permute-start(bf16[512,1024]{1,0:T(8,128)(2,1)} %refs_0_), channel_id=1, source_target_pairs={{4,8},{8,4},{0,0},{12,12},{5,9},{9,5},{1,1},{13,13},{6,10},{10,6},... | collective-permute-start | bytes 3145736 | tf_op jit(solution)/shard_map/ppermute | solution.py:287
  2.0 30.3 %collective-permute-start.4 = (bf16[512,1024]{1,0:T(8,128)(2,1)}, bf16[512,1024]{1,0:T(8,128)(2,1)S(1)}, u32[]{:S(2)}, u32[]{:S(2)}) collective-permute-start(bf16[512,1024]{1,0:T(8,128)(2,1)} %refs_0_), channel_id=1, source_target_pairs={{0,4},{4,0},{8,12},{12,8},{1,5},{5,1},{9,13},{13,9},{2,6},{6,2},{1... | collective-permute-start | bytes 3145736 | tf_op jit(solution)/shard_map/ppermute | solution.py:287
  8.1 24.2 %collective-permute-start.5 = (bf16[64,512]{1,0:T(8,128)(2,1)S(1)}, bf16[64,512]{1,0:T(8,128)(2,1)S(1)}, u32[]{:S(2)}, u32[]{:S(2)}) collective-permute-start(bf16[64,512]{1,0:T(8,128)(2,1)S(1)} %get-tuple-element.35), channel_id=1, source_target_pairs={{0,4},{4,0},{8,12},{12,8},{1,5},{5,1},{9,13},{13,9},{2,6},{6,2},{1... | collective-permute-start | bytes 196616 | tf_op jit(solution)/shard_map/ppermute | solution.py:287
  10.6 2.0 %copy-start.3 = (bf16[512,3584]{1,0:T(8,128)(2,1)S(1)}, bf16[512,3584]{1,0:T(8,128)(2,1)}, u32[]{:S(2)}) copy-start(bf16[512,3584]{1,0:T(8,128)(2,1)} %gate_ref) | copy-start | bytes 11010052
  12.7 5.4 %copy-start.5 = (bf16[512,1024]{1,0:T(8,128)(2,1)S(1)}, bf16[512,1024]{1,0:T(8,128)(2,1)}, u32[]{:S(2)}) copy-start(bf16[512,1024]{1,0:T(8,128)(2,1)} %refs_0_) | copy-start | bytes 3145732
  15.2 2.9 %copy-start.2 = (f32[3584,512]{1,0:T(8,128)}, f32[3584,512]{1,0:T(8,128)S(1)}, u32[]{:S(2)}) copy-start(f32[3584,512]{1,0:T(8,128)S(1)} %shard_map.109.refs_3_.factor_ref) | copy-start | bytes 22020100
  18.1 14.2 %copy-start.7 = (bf16[64,4096]{1,0:T(8,128)(2,1)S(1)}, bf16[64,4096]{1,0:T(8,128)(2,1)}, u32[]{:S(2)}) copy-start(bf16[64,4096]{1,0:T(8,128)(2,1)} %param.18) | copy-start | bytes 1572868
  24.6 19.5 %collective-permute-start.2 = (bf16[256,1024]{1,0:T(8,128)(2,1)S(1)}, bf16[256,1024]{1,0:T(8,128)(2,1)S(1)}, u32[]{:S(2)}, u32[]{:S(2)}) collective-permute-start(bf16[256,1024]{1,0:T(8,128)(2,1)S(1)} %get-tuple-element.33), channel_id=1, source_target_pairs={{0,8},{8,12},{12,4},{4,0},{1,9},{9,13},{13,5},{5,1},{2,10},{10,14}... | collective-permute-start | bytes 1572872 | tf_op jit(solution)/shard_map/ppermute | solution.py:287
  31.3 24.1 %collective-permute-start.1 = (bf16[256,1024]{1,0:T(8,128)(2,1)S(1)}, bf16[256,1024]{1,0:T(8,128)(2,1)S(1)}, u32[]{:S(2)}, u32[]{:S(2)}) collective-permute-start(bf16[256,1024]{1,0:T(8,128)(2,1)S(1)} %get-tuple-element.34), channel_id=1, source_target_pairs={{0,8},{8,12},{12,4},{4,0},{1,9},{9,13},{13,5},{5,1},{2,10},{10,14}... | collective-permute-start | bytes 1572872 | tf_op jit(solution)/shard_map/ppermute | solution.py:287
  32.3 25.0 %collective-permute-start.8 = (bf16[64,4096]{1,0:T(8,128)(2,1)S(1)}, bf16[64,4096]{1,0:T(8,128)(2,1)S(1)}, u32[]{:S(2)}, u32[]{:S(2)}) collective-permute-start(bf16[64,4096]{1,0:T(8,128)(2,1)S(1)} %copy-done.7), channel_id=1, source_target_pairs={{0,2},{2,0},{1,3},{3,1},{4,6},{6,4},{5,7},{7,5},{8,10},{10,8},{9,1... | collective-permute-start | bytes 1572872 | tf_op jit(solution)/shard_map/ppermute | solution.py:264
  35.2 35.7 %collective-permute-start.7 = (bf16[64,512]{1,0:T(8,128)(2,1)S(1)}, bf16[64,512]{1,0:T(8,128)(2,1)S(1)}, u32[]{:S(2)}, u32[]{:S(2)}) collective-permute-start(bf16[64,512]{1,0:T(8,128)(2,1)S(1)} %get-tuple-element.31), channel_id=1, source_target_pairs={{0,12},{12,0},{4,8},{8,4},{1,13},{13,1},{5,9},{9,5},{2,14},{14,2},... | collective-permute-start | bytes 196616 | tf_op jit(solution)/shard_map/ppermute | solution.py:287
  37.4 19.9 %copy-start.8 = (s32[256]{0:T(256)S(1)}, s32[256]{0:T(256)}, u32[]{:S(2)}) copy-start(s32[256]{0:T(256)} %param.19) | copy-start | bytes 3076
  44.0 23.5 %collective-permute-start.6 = (bf16[256,1024]{1,0:T(8,128)(2,1)S(1)}, bf16[256,1024]{1,0:T(8,128)(2,1)S(1)}, u32[]{:S(2)}, u32[]{:S(2)}) collective-permute-start(bf16[256,1024]{1,0:T(8,128)(2,1)S(1)} %collective-permute-done.2), channel_id=1, source_target_pairs={{0,4},{4,0},{8,12},{12,8},{1,5},{5,1},{9,13},{13,9},{2,6},{6,2},{1... | collective-permute-start | bytes 1572872 | tf_op jit(solution)/shard_map/ppermute | solution.py:287
  55.4 22.1 %collective-permute-start.3 = (bf16[256,1024]{1,0:T(8,128)(2,1)S(1)}, bf16[256,1024]{1,0:T(8,128)(2,1)S(1)}, u32[]{:S(2)}, u32[]{:S(2)}) collective-permute-start(bf16[256,1024]{1,0:T(8,128)(2,1)S(1)} %collective-permute-done.1), channel_id=1, source_target_pairs={{0,4},{4,0},{8,12},{12,8},{1,5},{5,1},{9,13},{13,9},{2,6},{6,2},{1... | collective-permute-start | bytes 1572872 | tf_op jit(solution)/shard_map/ppermute | solution.py:287
  58.2 9.4 %slice-start = ((s8[7340032]{0:T(1024)(128)(4,1)}), s8[4194304]{0:T(1024)(128)(4,1)S(1)}, s32[]{:S(2)}) async-start(s8[7340032]{0:T(1024)(128)(4,1)} %bitcast.4), calls=%async_computation | async-start | bytes 8388608
  58.2 9.4 %slice-start.1 = ((s8[7340032]{0:T(1024)(128)(4,1)}), s8[3145728]{0:T(1024)(128)(4,1)S(1)}, s32[]{:S(2)}) async-start(s8[7340032]{0:T(1024)(128)(4,1)} %bitcast.4), calls=%async_computation.1 | async-start | bytes 6291456
  58.2 9.4 %copy-start.4 = (bf16[3584,64]{0,1:T(8,128)(2,1)S(1)}, bf16[3584,64]{0,1:T(8,128)(2,1)}, u32[]{:S(2)}) copy-start(bf16[3584,64]{0,1:T(8,128)(2,1)} %param.16) | copy-start | bytes 1376260
  67.6 3.3 %copy-start.6 = (s32[1,512]{1,0:T(1,128)S(1)}, s32[1,512]{1,0:T(1,128)}, u32[]{:S(2)}) copy-start(s32[1,512]{1,0:T(1,128)} %seg_ref.1) | copy-start | bytes 6148
  77.5 13.8 %copy-start.1 = (bf16[512,1024]{1,0:T(8,128)(2,1)S(1)}, bf16[512,1024]{1,0:T(8,128)(2,1)}, u32[]{:S(2)}) copy-start(bf16[512,1024]{1,0:T(8,128)(2,1)} %param.12) | copy-start | bytes 3145732
  81.5 1.2 %collective-permute-start.9 = (f32[4,256]{1,0:T(4,128)S(1)}, f32[4,256]{1,0:T(4,128)S(1)}, u32[]{:S(2)}, u32[]{:S(2)}) collective-permute-start(f32[4,256]{1,0:T(4,128)S(1)} %shard_map.115), channel_id=1, source_target_pairs={{0,1},{1,0},{2,3},{3,2},{4,5},{5,4},{6,7},{7,6},{8,9},{9,8},{10,11... | collective-permute-start | bytes 12296 | tf_op jit(solution)/shard_map/ppermute | solution.py:23
  82.7 3.6 %collective-permute-start.10 = (f32[4,256]{1,0:T(4,128)S(1)}, f32[4,256]{1,0:T(4,128)S(1)}, u32[]{:S(2)}, u32[]{:S(2)}) collective-permute-start(f32[4,256]{1,0:T(4,128)S(1)} %add.44), channel_id=1, source_target_pairs={{0,4},{4,0},{8,12},{12,8},{1,5},{5,1},{9,13},{13,9},{2,6},{6,2},{1... | collective-permute-start | bytes 12296 | tf_op jit(solution)/shard_map/ppermute | solution.py:23
  86.3 4.5 %collective-permute-start.11 = (f32[4,256]{1,0:T(4,128)S(1)}, f32[4,256]{1,0:T(4,128)S(1)}, u32[]{:S(2)}, u32[]{:S(2)}) collective-permute-start(f32[4,256]{1,0:T(4,128)S(1)} %add.45), channel_id=1, source_target_pairs={{0,8},{4,12},{8,0},{12,4},{1,9},{5,13},{9,1},{13,5},{2,10},{6,14},... | collective-permute-start | bytes 12296 | tf_op jit(solution)/shard_map/ppermute | solution.py:23
